TPU v7x, 32 devices: a whole 2x2x4 slice. The times are simulated.
32 devices in a mesh: dp: 4 (over y, core), tile: 8 (over z, x).
Axes of the slice: x: 2, y: 2, z: 4, core: 2. Of those that a mesh axis runs over, the one named last changes fastest.
Arguments:
- inputs: bfloat16 [8, 64, 128, 256], P('dp', None, 'tile'), may hold values from -6 to 6
- cotangent: bfloat16 [8, 64, 128, 256], P('dp', None, 'tile'), may hold values from -6 to 6
- mode_weight: bfloat16 [64, 64, 64, 128], P('tile'), may hold values from -0.5 to 0.5
- local_weight: bfloat16 [64, 64], replicated, may hold values from -0.75 to 0.75
Outputs:
- input_grad: bfloat16 [8, 64, 128, 256], P('dp', None, 'tile')
- mode_grad: float32 [64, 64, 64, 128], P('tile')
- local_grad: float32 [64, 64], replicated
All inputs are finite; a program needn't handle non-finite values.
Results may differ from a plain program's by a relative error of at most 0.015.
Values may be sent and summed in bfloat16 or wider, within the bound.
No kernel may reach another device: no remote copies, remote signals or barrier semaphores. Data moves between devices by JAX's collectives and lax.ppermute only.
A program may use at most 128 MiB of HBM per device.

v0:
```python
import functools
import math

import jax
import jax.numpy as jnp
import numpy as np
from jax import lax
from jax.experimental import pallas as pl
from jax.experimental.pallas import tpu as pltpu
from jax.sharding import PartitionSpec as P

F32 = jnp.float32
BF16 = jnp.bfloat16
LIMIT = 56 * 1024 * 1024
SMALL = 24 * 1024 * 1024
ROWS = 8
PACK = 16
GROUP = 8
SPLIT = 4


def row_tables(height, modes):
    index = np.arange(modes)
    signed = np.where(index < modes // 2, index, index - modes)
    phases = np.mod(np.arange(height)[:, None] * signed[None, :], height)
    angles = phases * (2.0 * math.pi / height)
    return np.cos(angles), np.sin(angles)


def column_tables(width, modes):
    phases = np.mod(np.arange(modes)[:, None] * np.arange(width)[None, :], width)
    angles = phases * (2.0 * math.pi / width)
    return np.stack([np.cos(angles), -np.sin(angles)])


def constant(table):
    return jnp.asarray(np.asarray(table, np.float32)).astype(BF16)


def tables(tiles, owned, th, width, modes):
    cols = column_tables(width, tiles * owned)
    split = cols.reshape(2, tiles, owned, width)
    send_cols = split.transpose(1, 0, 2, 3).reshape(tiles, 2 * owned, width)
    send_cols = np.pad(send_cols, ((0, 0), (0, padded(2 * owned) - 2 * owned), (0, 0))).reshape(-1, width)
    back_cols = split.transpose(2, 1, 0, 3).reshape(-1, width)
    cosine, sine = row_tables(th * tiles, modes)
    real = np.concatenate([cosine, -sine], axis=1)
    imag = np.concatenate([sine, cosine], axis=1)
    pair = np.stack([real, imag]).reshape(2, tiles, th, 2 * modes)
    rows = pair.transpose(2, 1, 0, 3).reshape(-1, 2 * modes)
    back_rows = pair.transpose(1, 0, 2, 3).reshape(-1, 2 * modes)
    return constant(send_cols), constant(rows), constant(back_rows), constant(back_cols)


def padded(rows):
    return -(-rows // PACK) * PACK


def order(outer, inner):
    take = np.arange(outer * inner).reshape(outer, inner).T.reshape(-1)
    return constant(np.eye(outer * inner)[take])


def mode_order(tiles, owned):
    rows = np.arange(tiles * padded(2 * owned)).reshape(tiles, -1)
    take = rows[:, : 2 * owned].reshape(tiles, 2, owned).transpose(2, 0, 1).reshape(-1)
    return constant(np.eye(rows.size)[take])


def dot(left, right, dims):
    return lax.dot_general(left, right, (dims, ((), ())), preferred_element_type=F32)


def low_half(shape, half):
    return lax.broadcasted_iota(jnp.int32, shape, 1) < half


def gelu_slope(values):
    size = jnp.abs(values)
    expo = jnp.exp(-0.5 * values * values)
    t = 1.0 / (1.0 + (0.3275911 / math.sqrt(2.0)) * size)
    poly = 0.5 * 1.061405429
    for factor in (-1.453152027, 1.421413741, -0.284496736, 0.254829592):
        poly = poly * t + 0.5 * factor
    tail = poly * t * expo
    cumulative = jnp.where(values < 0.0, tail, 1.0 - tail)
    return cumulative + values * expo * (1.0 / math.sqrt(2.0 * math.pi))


def shuffle(order_ref, value):
    return dot(order_ref[...], value, ((1,), (0,))).astype(BF16)


def by_rows(order_ref, field_refs, rows_ref):
    heights, lanes, _ = rows_ref.shape
    block = PACK * heights
    quarter = lanes // len(field_refs)
    for first in range(0, lanes, PACK):
        start = first % quarter * heights
        moved = shuffle(order_ref, field_refs[first // quarter][start : start + block, :])
        for h in range(heights):
            rows_ref[h, first : first + PACK, :] = moved[h * PACK : (h + 1) * PACK]


def columns_kernel(order_ref, table_ref, *rest):
    field_refs, (rows_ref, send_ref) = rest[:SPLIT], rest[SPLIT:]
    heights, lanes, _ = rows_ref.shape
    by_rows(order_ref, field_refs, rows_ref)
    for h in range(heights):
        send_ref[:, h * lanes : (h + 1) * lanes] = dot(table_ref[...], rows_ref[h], ((1,), (1,))).astype(BF16)


def relayout_kernel(order_ref, *rest):
    by_rows(order_ref, rest[:SPLIT], rest[SPLIT])


def shuffle_groups(order_ref, recv_ref):
    size = order_ref.shape[0]
    return [shuffle(order_ref, recv_ref[n : n + size, :]) for n in range(0, recv_ref.shape[0], size)]


def stack(groups, index, count, lanes):
    return jnp.concatenate(
        [
            group[index * count : (index + 1) * count, n : n + lanes]
            for n in range(0, groups[0].shape[1], lanes)
            for group in groups
        ],
        axis=0,
    )


def spectra_into(scale, owned, recv_ref, order_ref, rows_ref, spec_ref):
    count = order_ref.shape[0] // owned
    lanes = recv_ref.shape[1] * count // rows_ref.shape[0]
    ordered = [shuffle(order_ref, recv_ref[...])]
    for q in range(owned):
        stacked = stack(ordered, q, count, lanes)
        spec_ref[q * lanes : (q + 1) * lanes, :] = (
            scale * dot(stacked, rows_ref[...], ((0,), (0,)))
        ).astype(BF16)


def grad_spectra_kernel(scale, owned, recv_ref, order_ref, rows_ref, local_ref, spec_ref):
    spectra_into(scale, owned, recv_ref, order_ref, rows_ref, spec_ref)
    value = local_ref[...]
    high = value.astype(BF16)
    low = (value - high.astype(F32)).astype(BF16)
    spec_ref[spec_ref.shape[0] - value.shape[0] :, :] = jnp.concatenate([high, low], axis=1)


def tree(terms):
    while len(terms) > 1:
        terms = [a + b for a, b in zip(terms[0::2], terms[1::2])]
    return terms[0]


def rows_of(store, block, extent):
    return store.at[pl.ds(pl.multiple_of(block * extent, extent), extent), :]


def packed_row(view, index):
    row = view[index : index + 1, :]
    return jnp.broadcast_to(row, (PACK, row.shape[1])).astype(BF16)


def duplicates(spec, half):
    value = spec.astype(F32)
    other = pltpu.roll(value, half, 1)
    low = low_half(value.shape, half)
    return jnp.where(low, value, other), jnp.where(low, other, value)


def finish(back_ref, sums, send_ref, mix):
    @pl.when(pl.program_id(0) == pl.num_programs(0) - 1)
    def _():
        owned = sums.shape[0]
        lanes = send_ref.shape[1] // owned
        for q in range(owned):
            mixed = mix(sums.at[q]).astype(BF16)
            send_ref[:, q * lanes : (q + 1) * lanes] = dot(back_ref[...], mixed, ((1,), (1,))).astype(BF16)


def forward_kernel(scale, samples, owned, recv_ref, order_ref, rows_ref, back_ref, weight_ref, *rest):
    spec_ref, send_ref, real, imag, sums = rest
    _, _, outs, both = sums.shape
    channels = weight_ref.shape[0] // outs
    half = both // 2
    lanes = samples * channels
    q = pl.program_id(0)

    @pl.when(q == 0)
    def _():
        spectra_into(scale, owned, recv_ref, order_ref, rows_ref, spec_ref)
        real[...], imag[...] = duplicates(spec_ref[...], half)
        sums[...] = jnp.zeros_like(sums)

    def body(block, carry):
        view = rows_of(weight_ref, block, GROUP * outs)
        rows = []
        for s in range(samples):
            for store in (real, imag):
                part = rows_of(store, (q * lanes + s * channels) // GROUP + block, GROUP)
                rows.append([packed_row(part, step) for step in range(GROUP)])
        into = sums.at[q]
        for start in range(0, outs, 2 * PACK):
            totals = []
            for o in (start, start + PACK):
                column = [view[step * outs + o : step * outs + o + PACK, :] for step in range(GROUP)]
                for n, row in enumerate(rows):
                    totals.append((n, o, tree([w * r for w, r in zip(column, row)])))
            updated = [(n, o, into[n, o : o + PACK, :] + total.astype(F32)) for n, o, total in totals]
            for n, o, total in updated:
                into[n, o : o + PACK, :] = total
        return carry

    lax.fori_loop(0, channels // GROUP, body, 0)

    def mix(parts):
        low = low_half((outs, both), half)
        result = []
        for s in range(samples):
            crossed = pltpu.roll(parts[2 * s + 1], half, 1)
            result.append(parts[2 * s] + jnp.where(low, -crossed, crossed))
        return jnp.concatenate(result, axis=0)

    finish(back_ref, sums, send_ref, mix)


def backward_kernel(samples, spec_ref, back_ref, weight_ref, send_ref, real, imag, sums):
    channels, both = sums.shape[2] // ROWS, sums.shape[3]
    outs = weight_ref.shape[0] // channels
    half = both // 2
    lanes = samples * outs
    q = pl.program_id(0)

    @pl.when(q == 0)
    def _():
        first, second = duplicates(spec_ref[: real.shape[0], :], half)
        real[...], imag[...] = first.astype(BF16), second.astype(BF16)

    grads = [
        [store[pl.ds(pl.multiple_of(q * lanes + s * outs + o, PACK), PACK), :] for o in range(0, outs, PACK)]
        for s in range(samples)
        for store in (real, imag)
    ]

    def body(block, carry):
        view = rows_of(weight_ref, block, GROUP * outs)
        totals = []
        for step in range(GROUP):
            column = [view[step * outs + o : step * outs + o + PACK, :] for o in range(0, outs, PACK)]
            for n, grad in enumerate(grads):
                total = tree([w * g for w, g in zip(column, grad)]).astype(F32)
                totals.append((n, step, total[:ROWS] + total[ROWS:]))
        into = [rows_of(sums.at[q, n], block, GROUP * ROWS) for n in range(len(grads))]
        for n, step, total in totals:
            into[n][step * ROWS : (step + 1) * ROWS, :] = total
        return carry

    lax.fori_loop(0, channels // GROUP, body, 0)

    def mix(parts):
        low = low_half((channels, both), half)
        result = []
        for s in range(samples):
            straight, crossed = (
                sum(parts[n, pl.ds(row, channels, stride=ROWS), :] for row in range(ROWS)) for n in (2 * s, 2 * s + 1)
            )
            result.append(jnp.where(low, straight, -straight) + pltpu.roll(crossed, half, 1))
        return jnp.concatenate(result, axis=0)

    finish(back_ref, sums, send_ref, mix)


def pixels_kernel(scale, heights, recv_ref, order_ref, back_ref, local_ref, field_ref, cot_ref, table_ref, *rest):
    grad_ref, send_ref, sum_ref, ordered, total = rest
    steps, lanes, _ = field_ref.shape
    count = order_ref.shape[0] // heights
    size = order_ref.shape[0]
    group = pl.program_id(0)

    @pl.when(group == 0)
    def _():
        for n in range(0, recv_ref.shape[0], size):
            ordered[n : n + size, :] = shuffle(order_ref, recv_ref[n : n + size, :])
        total[...] = jnp.zeros_like(total)

    local = jnp.zeros(total.shape, F32)
    for step in range(steps):
        parts = []
        for n in range(0, recv_ref.shape[0], size):
            first = pl.multiple_of(n + (group * steps + step) * count, count)
            parts.append(ordered[pl.ds(first, count), :])
        inner = stack(parts, 0, count, lanes)
        pre = scale * dot(inner, back_ref[...], ((0,), (0,)))
        pre = pre + dot(local_ref[...], field_ref[step], ((1,), (0,)))
        grad = (cot_ref[step].astype(F32) * gelu_slope(pre)).astype(BF16)
        grad_ref[step] = grad
        send_ref[:, step * lanes : (step + 1) * lanes] = dot(table_ref[...], grad, ((1,), (1,))).astype(BF16)
        local = local + dot(field_ref[step], grad, ((1,), (1,)))
    total[...] += local

    @pl.when(group == pl.num_programs(0) - 1)
    def _():
        extent = sum_ref.shape[0]
        sum_ref[...] = sum(total[n : n + extent, n : n + extent] for n in range(0, lanes, extent))


def final_kernel(scale, recv_ref, order_ref, back_ref, local_ref, grad_ref, restore_ref, out_ref, result):
    heights, lanes, _ = grad_ref.shape
    count = order_ref.shape[0] // heights
    ordered = shuffle_groups(order_ref, recv_ref)
    for h in range(heights):
        inner = stack(ordered, h, count, lanes)
        value = scale * dot(inner, back_ref[...], ((0,), (0,)))
        result[h] = (value + dot(local_ref[...], grad_ref[h], ((1,), (0,)))).astype(BF16)
    block = PACK * heights
    for first in range(0, lanes, PACK):
        part = jnp.concatenate([result[h, first : first + PACK, :] for h in range(heights)], axis=0)
        out_ref[first * heights : first * heights + block, :] = shuffle(restore_ref, part)


def outer_kernel(samples, groups, *refs):
    specs, grads, pairs = refs[:groups], refs[groups : 2 * groups], refs[2 * groups : 3 * groups]
    out_ref, local_ref, real, imag, plain, crossed = refs[3 * groups :]
    total, channels, both = real.shape
    outs = plain.shape[1]
    half = both // 2
    low = low_half((channels, both), half)

    @pl.when(pl.program_id(0) == 0)
    def _():
        value = 0.0
        for pair_ref in pairs:
            pair = pair_ref[...].astype(F32)
            value = value + pair[:, :channels] + pair[:, channels : 2 * channels]
        local_ref[...] = value

    for g in range(groups):
        for s in range(samples):
            n = g * samples + s
            spec = specs[g][s * channels : (s + 1) * channels, :].astype(F32)
            other = pltpu.roll(spec, half, 1)
            real[n] = jnp.where(low, spec, other)
            imag[n] = jnp.where(low, other, -spec)
            grad = grads[g][s * outs : (s + 1) * outs, :]
            plain[n] = grad
            crossed[n] = pltpu.roll(grad.astype(F32), half, 1).astype(BF16)

    def body(block, carry):
        into = rows_of(out_ref, block, GROUP * outs)
        views = [rows_of(store.at[n], block, GROUP) for n in range(total) for store in (real, imag)]
        for first in range(0, GROUP, 2):
            pair = range(first, first + 2)
            lefts = [[packed_row(view, c) for view in views] for c in pair]
            results = []
            for o in range(0, outs, PACK):
                right = [store[n, o : o + PACK, :] for n in range(total) for store in (plain, crossed)]
                for c, left in zip(pair, lefts):
                    results.append((c * outs + o, tree([a * b for a, b in zip(left, right)])))
            for row, result in results:
                into[row : row + PACK, :] = result.astype(F32)
        return carry

    lax.fori_loop(0, channels // GROUP, body, 0)


def whole(extent):
    return pl.BlockSpec(extent, lambda *_: (0,) * len(extent))


def call(kernel, name, operands, outs, scratch=(), grid=(1,), blocks=None, out_blocks=None, limit=LIMIT):
    blocks, out_blocks = blocks or {}, out_blocks or {}
    in_specs = [blocks.get(n) or whole(operand.shape) for n, operand in enumerate(operands)]
    out_specs = [out_blocks.get(n, whole(out.shape)) for n, out in enumerate(outs)]
    return pl.pallas_call(
        kernel,
        out_shape=tuple(outs),
        grid=grid,
        in_specs=in_specs,
        out_specs=tuple(out_specs),
        scratch_shapes=list(scratch),
        compiler_params=pltpu.CompilerParams(vmem_limit_bytes=limit),
        name=name,
    )(*operands)


def gather(values, axis):
    size = lax.axis_size(axis)
    return [values] + [
        lax.ppermute(values, axis, [(i, i ^ step) for i in range(size)]) for step in range(1, size)
    ]


def sum_over(values, axis):
    size = lax.axis_size(axis)
    top = size
    while top > 1:
        low = max(top // 4, 1)
        values = sum(
            (lax.ppermute(values, axis, [(i, i ^ step) for i in range(size)]) for step in range(low, top, low)),
            values,
        )
        top = low
    return values


def block_diagonal(matrix, copies):
    zero = jnp.zeros_like(matrix)
    return jnp.concatenate(
        [
            jnp.concatenate([matrix if i == j else zero for j in range(copies)], axis=1)
            for i in range(copies)
        ],
        axis=0,
    )


def shape(extent, kind=BF16):
    return jax.ShapeDtypeStruct(extent, kind)


def local(inputs, cotangent, mode_weight, local_weight):
    tiles = lax.axis_size("tile")
    samples, channels, th, width = inputs.shape
    owned, _, _, both = mode_weight.shape
    modes = both // 2
    lanes = samples * channels
    parts = width // 128
    spec_scale = 1.0 / math.sqrt(tiles * th * width)
    mode_scale = 1.0 / math.sqrt(modes * tiles * owned)
    send_cols, rows, back_rows, back_cols = tables(tiles, owned, th, width, modes)
    pixel_rows = samples * channels * th
    halves = tiles * padded(2 * owned)
    inverse = 2 * tiles * th

    def exchange(values):
        split = values.reshape(tiles, values.shape[0] // tiles, values.shape[1])
        moved = lax.all_to_all(split, "tile", split_axis=0, concat_axis=0, tiled=False)
        return moved.reshape(values.shape)

    forward_mix = block_diagonal(local_weight.T, samples)
    backward_mix = block_diagonal(local_weight, samples)
    by_row = order(PACK, th)
    by_channel = order(th, PACK)
    by_mode = mode_order(tiles, owned)
    by_height = order(2 * min(tiles, 8), th)
    flat_weight = mode_weight.reshape(-1, both)
    weight_block = pl.BlockSpec((flat_weight.shape[0] // owned, both), lambda q: (q, 0))
    to_modes = shape((halves, th * lanes))
    to_pixels = shape((inverse, owned * lanes))
    field_shape = shape((th, lanes, width))

    def field_blocks(first):
        return {first + n: pl.BlockSpec((pixel_rows // SPLIT, width), lambda _, n=n: (n, 0)) for n in range(SPLIT)}

    field_rows, send = call(
        columns_kernel,
        "columns",
        (by_row, send_cols, *[inputs.reshape(pixel_rows, width)] * SPLIT),
        (field_shape, to_modes),
        blocks=field_blocks(2),
    )
    arrived = exchange(send)
    (cot_rows,) = call(
        relayout_kernel,
        "relayout",
        (by_row, *[cotangent.reshape(pixel_rows, width)] * SPLIT),
        (field_shape,),
        blocks=field_blocks(1),
    )
    spectra, send = call(
        functools.partial(forward_kernel, spec_scale, samples, owned),
        "mix_forward",
        (arrived, by_mode, rows, back_rows, flat_weight),
        (shape((owned * lanes, both)), to_pixels),
        [
            pltpu.VMEM((owned * lanes, both), F32),
            pltpu.VMEM((owned * lanes, both), F32),
            pltpu.VMEM((owned, 2 * samples, channels, both), F32),
        ],
        grid=(owned,),
        blocks={4: weight_block},
    )
    all_spectra = gather(spectra, "dp")
    arrived = exchange(send)
    arrived, *all_spectra = lax.optimization_barrier((arrived, *all_spectra))
    steps = 4
    row_block = pl.BlockSpec((steps, lanes, width), lambda n: (n, 0, 0))
    gate_rows, send, local_sum = call(
        functools.partial(pixels_kernel, mode_scale, th),
        "pixels",
        (arrived, by_height, back_cols, forward_mix, field_rows, cot_rows, send_cols),
        (field_shape, to_modes, shape((channels, channels), F32)),
        [pltpu.VMEM((inverse, owned * lanes), BF16), pltpu.VMEM((lanes, lanes), F32)],
        grid=(th // steps,),
        blocks={4: row_block, 5: row_block},
        out_blocks={0: row_block, 1: pl.BlockSpec((halves, steps * lanes), lambda n: (0, n))},
        limit=SMALL,
    )
    arrived = exchange(send)
    local_sum = sum_over(local_sum, "tile")
    (grad_spectra,) = call(
        functools.partial(grad_spectra_kernel, mode_scale, owned),
        "grad_spectra",
        (arrived, by_mode, rows, local_sum),
        (shape((owned * lanes + channels, both)),),
        limit=SMALL,
    )
    all_grads = gather(grad_spectra, "dp")
    (send,) = call(
        functools.partial(backward_kernel, samples),
        "mix_backward",
        (grad_spectra, back_rows, flat_weight),
        (to_pixels,),
        [
            pltpu.VMEM((owned * lanes, both), BF16),
            pltpu.VMEM((owned * lanes, both), BF16),
            pltpu.VMEM((owned, 2 * samples, channels * ROWS, both), F32),
        ],
        grid=(owned,),
        blocks={2: weight_block},
    )
    send, *all_grads = lax.optimization_barrier((send, *all_grads))
    arrived = exchange(send)

    groups = lax.axis_size("dp")
    total = groups * samples
    per_mode = pl.BlockSpec((lanes, both), lambda q: (q, 0))
    below = owned * lanes // channels
    pair_block = pl.BlockSpec((channels, both), lambda q: (below, 0))
    mode_grad, local_grad = call(
        functools.partial(outer_kernel, samples, groups),
        "mode_grad",
        (*all_spectra, *all_grads, *all_grads),
        (shape(flat_weight.shape, F32), shape((channels, channels), F32)),
        [pltpu.VMEM((total, channels, both), F32)] * 2 + [pltpu.VMEM((total, channels, both), BF16)] * 2,
        grid=(owned,),
        blocks={n: per_mode if n < 2 * groups else pair_block for n in range(3 * groups)},
        out_blocks={0: weight_block},
    )
    arrived, mode_grad = lax.optimization_barrier((arrived, mode_grad))

    (input_grad,) = call(
        functools.partial(final_kernel, spec_scale),
        "final",
        (arrived, by_height, back_cols, backward_mix, gate_rows, by_channel),
        (shape((pixel_rows, width)),),
        [pltpu.VMEM((th, lanes, width), BF16)],
        limit=SMALL,
    )
    return (input_grad.reshape(inputs.shape), mode_grad.reshape(mode_weight.shape), local_grad)


def solution(mesh):
    return jax.shard_map(
        local,
        mesh=mesh,
        in_specs=(
            P("dp", None, "tile", None),
            P("dp", None, "tile", None),
            P("tile", None, None, None),
            P(),
        ),
        out_specs=(P("dp", None, "tile", None), P("tile", None, None, None), P()),
        check_vma=False,
    )
```

profile of v0, /device:TPU:0, one launch (start us, length us, event | category | flops | bytes accessed | tf_op | source)
XLA Modules:
  0.0 129.0 jit_solution(5164881177517306217)
XLA Ops:
  0.6 0.0 copy-start.2
  0.6 0.0 copy-start.5
  0.7 0.0 copy-start.7
  0.7 0.0 copy-start.4
  0.7 0.0 copy-start.6
  0.7 3.0 %columns.1 = (bf16[16,128,256]{2,1,0:T(8,128)(2,1)}, bf16[128,2048]{1,0:T(8,128)(2,1)}) custom-call(bf16[256,256]{1,0:T(8,128)(2,1)} %constant.30.order_ref.restore_ref, bf16[128,256]{1,0:T(8,128)(2,1)} %constant.31.table_ref, bf16[2048,256]{1,0:T(8,128)(2,1)} %bitcast.19, bf16[2048,256]{1,0:T(8,128)(2,1)} %bitcast.20, bf16[2048,256]{1,0:T(8,128)(2,1)} %bitcast.21, ...), custom_call_target="tpu_custom_call" | custom-call | tf_op jit(solution)/shard_map/columns/pallas_call | solution.py:377
  3.7 22.0 %all_to_all.20 = bf16[8,16,2048]{2,1,0:T(8,128)(2,1)} all-to-all(bf16[8,16,2048]{2,1,0:T(8,128)(2,1)} %bitcast.31), channel_id=1, replica_groups=mesh['dp'=4,'tile'=8] {'tile'}, dimensions={0} | all-to-all | bytes 1048576 | tf_op jit(solution)/shard_map/all_to_all | solution.py:440
  25.7 11.0 %mix_forward.1 = (bf16[1024,128]{1,0:T(8,128)(2,1)}, bf16[256,1024]{1,0:T(8,128)(2,1)}) custom-call(bf16[128,2048]{1,0:T(8,128)(2,1)} %bitcast.28, bf16[128,128]{1,0:T(8,128)(2,1)} %constant.32.order_ref, bf16[256,128]{1,0:T(8,128)(2,1)} %constant.33.rows_ref, bf16[256,128]{1,0:T(8,128)(2,1)} %constant.34.back_ref, bf16[32768,128]{1,0:T(8,128)(2,1)} %bitcast.17), custom_call_target="tpu_custom_call" | custom-call | tf_op jit(solution)/shard_map/mix_forward/pallas_call | solution.py:377
  36.7 3.6 %all-to-all-start.1 = ((bf16[8,32,1024]{2,1,0:T(8,128)(2,1)}), bf16[8,32,1024]{2,1,0:T(8,128)(2,1)S(1)}, u32[]{:S(2)}, u32[]{:S(2)}) async-start(bf16[8,32,1024]{2,1,0:T(8,128)(2,1)} %bitcast.30), calls=%async_computation.1 | async-start | bytes 1048576 | tf_op jit(solution)/shard_map/all_to_all | solution.py:440
  40.3 0.0 collective-permute-start
  40.3 1.6 %collective-permute-start.1 = (bf16[1024,128]{1,0:T(8,128)(2,1)}, bf16[1024,128]{1,0:T(8,128)(2,1)S(1)}, u32[]{:S(2)}, u32[]{:S(2)}) collective-permute-start(bf16[1024,128]{1,0:T(8,128)(2,1)} %get-tuple-element.32.refs_0_), channel_id=1, source_target_pairs={{0,16},{8,24},{16,0},{24,8},{1,17},{9,25},{17,1},{25,9},{2,18},{10... | collective-permute-start | bytes 786440 | tf_op jit(solution)/shard_map/ppermute | solution.py:392
  41.9 0.3 collective-permute-start.2
  42.1 0.8 copy.15
  42.9 2.6 %relayout.1.cot_ref = bf16[16,128,256]{2,1,0:T(8,128)(2,1)} custom-call(bf16[256,256]{1,0:T(8,128)(2,1)} %constant.30.order_ref.restore_ref, bf16[2048,256]{1,0:T(8,128)(2,1)} %bitcast.23, bf16[2048,256]{1,0:T(8,128)(2,1)} %bitcast.24, bf16[2048,256]{1,0:T(8,128)(2,1)} %bitcast.25, bf16[2048,256]{1,0:T(8,128)(2,1)} %bitcast.26), custom_call_target="tpu_custom_call" | custom-call | tf_op jit(solution)/shard_map/relayout/pallas_call | solution.py:377
  45.6 0.1 fusion.4.local_ref
  45.7 0.0 collective-permute-done.refs_1_
  45.7 4.0 %collective-permute-done.1.refs_2_ = bf16[1024,128]{1,0:T(8,128)(2,1)S(1)} collective-permute-done((bf16[1024,128]{1,0:T(8,128)(2,1)}, bf16[1024,128]{1,0:T(8,128)(2,1)S(1)}, u32[]{:S(2)}, u32[]{:S(2)}) %collective-permute-start.1) | collective-permute-done | bytes 262176 | tf_op jit(solution)/shard_map/ppermute | solution.py:392
  49.7 4.7 %collective-permute-done.2.refs_3_ = bf16[1024,128]{1,0:T(8,128)(2,1)S(1)} collective-permute-done((bf16[1024,128]{1,0:T(8,128)(2,1)}, bf16[1024,128]{1,0:T(8,128)(2,1)S(1)}, u32[]{:S(2)}, u32[]{:S(2)}) %collective-permute-start.2) | collective-permute-done | bytes 262176 | tf_op jit(solution)/shard_map/ppermute | solution.py:392
  54.4 0.1 all-to-all-done.1
  54.4 0.0 copy-done.12
  54.4 0.6 copy-done.13
  55.1 0.0 copy-start.1
  55.1 1.2 copy-done.1
  56.3 6.6 %pixels.1 = (bf16[16,128,256]{2,1,0:T(8,128)(2,1)S(1)}, bf16[128,2048]{1,0:T(8,128)(2,1)}, f32[64,64]{1,0:T(8,128)S(1)}) custom-call(bf16[256,1024]{1,0:T(8,128)(2,1)S(1)} %bitcast.15, bf16[256,256]{1,0:T(8,128)(2,1)S(1)} %copy-done.2, bf16[128,256]{1,0:T(8,128)(2,1)S(1)} %copy-done.6, bf16[128,128]{1,0:T(8,128)(2,1)S(1)} %fusion.4.local_ref, ...), custom_call_target="tpu_custom_call" | custom-call | tf_op jit(solution)/shard_map/pixels/pallas_call | solution.py:377
  63.0 6.0 %all-to-all-start.2 = ((bf16[8,16,2048]{2,1,0:T(8,128)(2,1)}), bf16[8,16,2048]{2,1,0:T(8,128)(2,1)S(1)}, u32[]{:S(2)}, u32[]{:S(2)}) async-start(bf16[8,16,2048]{2,1,0:T(8,128)(2,1)} %bitcast.8), calls=%async_computation.2 | async-start | bytes 1048576 | tf_op jit(solution)/shard_map/all_to_all | solution.py:440
  69.0 3.8 %collective-permute-start.5 = (f32[64,64]{1,0:T(8,128)S(1)}, f32[64,64]{1,0:T(8,128)S(1)}, u32[]{:S(2)}, u32[]{:S(2)}) collective-permute-start(f32[64,64]{1,0:T(8,128)S(1)} %get-tuple-element.30), channel_id=1, source_target_pairs={{0,6},{1,7},{2,4},{3,5},{4,2},{5,3},{6,0},{7,1},{8,14},{9,15},{10,... | collective-permute-start | bytes 49160 | tf_op jit(solution)/shard_map/ppermute | solution.py:402
  72.8 0.0 collective-permute-start.4
  72.8 0.6 collective-permute-start.3
  73.4 9.9 %collective-permute-done.5 = f32[64,64]{1,0:T(8,128)S(1)} collective-permute-done((f32[64,64]{1,0:T(8,128)S(1)}, f32[64,64]{1,0:T(8,128)S(1)}, u32[]{:S(2)}, u32[]{:S(2)}) %collective-permute-start.5) | collective-permute-done | bytes 16416 | tf_op jit(solution)/shard_map/ppermute | solution.py:402
  83.4 3.3 %collective-permute-done.4 = f32[64,64]{1,0:T(8,128)S(1)} collective-permute-done((f32[64,64]{1,0:T(8,128)S(1)}, f32[64,64]{1,0:T(8,128)S(1)}, u32[]{:S(2)}, u32[]{:S(2)}) %collective-permute-start.4) | collective-permute-done | bytes 16416 | tf_op jit(solution)/shard_map/ppermute | solution.py:402
  86.7 0.0 collective-permute-done.3
  86.7 1.5 %collective-permute-start.6 = (f32[64,64]{1,0:T(8,128)S(1)}, f32[64,64]{1,0:T(8,128)S(1)}, u32[]{:S(2)}, u32[]{:S(2)}) collective-permute-start(f32[64,64]{1,0:T(8,128)S(1)} %add_add_fusion), channel_id=1, source_target_pairs={{0,1},{1,0},{2,3},{3,2},{4,5},{5,4},{6,7},{7,6},{8,9},{9,8},{10,11... | collective-permute-start | bytes 49160 | tf_op jit(solution)/shard_map/ppermute | solution.py:402
  88.2 2.5 %collective-permute-done.6 = f32[64,64]{1,0:T(8,128)S(1)} collective-permute-done((f32[64,64]{1,0:T(8,128)S(1)}, f32[64,64]{1,0:T(8,128)S(1)}, u32[]{:S(2)}, u32[]{:S(2)}) %collective-permute-start.6) | collective-permute-done | bytes 16416 | tf_op jit(solution)/shard_map/ppermute | solution.py:402
  90.7 0.0 all-to-all-done.2
  90.7 0.6 grad_spectra.1.spec_ref.refs_4_.refs_8_
  91.3 0.1 collective-permute-start.7
  91.4 1.6 %collective-permute-start.8 = (bf16[1088,128]{1,0:T(8,128)(2,1)S(1)}, bf16[1088,128]{1,0:T(8,128)(2,1)S(1)}, u32[]{:S(2)}, u32[]{:S(2)}) collective-permute-start(bf16[1088,128]{1,0:T(8,128)(2,1)S(1)} %grad_spectra.1.spec_ref.refs_4_.refs_8_), channel_id=1, source_target_pairs={{0,16},{8,24},{16,0},{24,8},{1,17},{9,25},{17,1},{25,9},{2,18},{10... | collective-permute-start | bytes 835592 | tf_op jit(solution)/shard_map/ppermute | solution.py:392
  93.0 0.3 collective-permute-start.9
  93.3 10.7 %mix_backward.1 = bf16[256,1024]{1,0:T(8,128)(2,1)} custom-call(bf16[1088,128]{1,0:T(8,128)(2,1)} %copy-done, bf16[256,128]{1,0:T(8,128)(2,1)} %constant.34.back_ref, bf16[32768,128]{1,0:T(8,128)(2,1)} %bitcast.18), custom_call_target="tpu_custom_call" | custom-call | tf_op jit(solution)/shard_map/mix_backward/pallas_call | solution.py:377
  103.9 0.0 collective-permute-done.7.refs_5_.refs_9_
  103.9 0.0 collective-permute-done.8.refs_6_.refs_10_
  104.0 2.0 %collective-permute-done.9.refs_7_.refs_11_ = bf16[1088,128]{1,0:T(8,128)(2,1)S(1)} collective-permute-done((bf16[1088,128]{1,0:T(8,128)(2,1)S(1)}, bf16[1088,128]{1,0:T(8,128)(2,1)S(1)}, u32[]{:S(2)}, u32[]{:S(2)}) %collective-permute-start.9) | collective-permute-done | bytes 278560 | tf_op jit(solution)/shard_map/ppermute | solution.py:392
  106.0 3.6 %all-to-all-start.3 = ((bf16[8,32,1024]{2,1,0:T(8,128)(2,1)}), bf16[8,32,1024]{2,1,0:T(8,128)(2,1)S(1)}, u32[]{:S(2)}, u32[]{:S(2)}) async-start(bf16[8,32,1024]{2,1,0:T(8,128)(2,1)} %bitcast.27), calls=%async_computation.3 | async-start | bytes 1048576 | tf_op jit(solution)/shard_map/all_to_all | solution.py:440
  109.6 0.1 fusion.5.local_ref
  109.7 0.0 copy-done.11
  109.7 17.0 %mode_grad.1 = (f32[32768,128]{1,0:T(8,128)}, f32[64,64]{1,0:T(8,128)}) custom-call(bf16[1024,128]{1,0:T(8,128)(2,1)} %get-tuple-element.32.refs_0_, bf16[1024,128]{1,0:T(8,128)(2,1)} %copy-done.11, bf16[1024,128]{1,0:T(8,128)(2,1)} %copy-done.12, bf16[1024,128]{1,0:T(8,128)(2,1)} %copy-done.13, bf16[1088,128]{1,0:T(8,128)(2,1)} %copy-done, ...), custom_call_target="tpu_custom_call" | custom-call | tf_op jit(solution)/shard_map/mode_grad/pallas_call | solution.py:377
  126.7 0.0 all-to-all-done.3
  126.7 2.3 %final.1 = bf16[2048,256]{1,0:T(8,128)(2,1)} custom-call(bf16[256,1024]{1,0:T(8,128)(2,1)S(1)} %bitcast.16, bf16[256,256]{1,0:T(8,128)(2,1)S(1)} %copy-done.2, bf16[128,256]{1,0:T(8,128)(2,1)S(1)} %copy-done.6, bf16[128,128]{1,0:T(8,128)(2,1)S(1)} %fusion.5.local_ref, bf16[16,128,256]{2,1,0:T(8,128)(2,1)S(1)} %get-tuple-element.42.grad_ref, ...), custom_call_target="tpu_custom_call" | custom-call | tf_op jit(solution)/shard_map/final/pallas_call | solution.py:377
  (22 shorter events, 0.1 us)
Async XLA Ops:
  0.6 54.5 %copy-start.2 = (bf16[256,256]{1,0:T(8,128)(2,1)S(1)}, bf16[256,256]{1,0:T(8,128)(2,1)}, u32[]{:S(2)}) copy-start(bf16[256,256]{1,0:T(8,128)(2,1)} %constant.30.order_ref.restore_ref) | copy-start | bytes 393220
  0.6 54.5 %copy-start.5 = (bf16[128,256]{1,0:T(8,128)(2,1)S(1)}, bf16[128,256]{1,0:T(8,128)(2,1)}, u32[]{:S(2)}) copy-start(bf16[128,256]{1,0:T(8,128)(2,1)} %constant.31.table_ref) | copy-start | bytes 196612
  0.7 90.0 %copy-start.7 = (bf16[128,128]{1,0:T(8,128)(2,1)S(1)}, bf16[128,128]{1,0:T(8,128)(2,1)}, u32[]{:S(2)}) copy-start(bf16[128,128]{1,0:T(8,128)(2,1)} %constant.32.order_ref) | copy-start | bytes 98308
  0.7 90.0 %copy-start.4 = (bf16[256,128]{1,0:T(8,128)(2,1)S(1)}, bf16[256,128]{1,0:T(8,128)(2,1)}, u32[]{:S(2)}) copy-start(bf16[256,128]{1,0:T(8,128)(2,1)} %constant.33.rows_ref) | copy-start | bytes 196612
  0.7 54.4 %copy-start.6 = (bf16[128,256]{1,0:T(8,128)(2,1)S(1)}, bf16[128,256]{1,0:T(8,128)(2,1)}, u32[]{:S(2)}) copy-start(bf16[128,256]{1,0:T(8,128)(2,1)} %constant.35.back_ref) | copy-start | bytes 196612
  3.6 51.5 %copy-start.3 = (bf16[16,128,256]{2,1,0:T(8,128)(2,1)S(1)}, bf16[16,128,256]{2,1,0:T(8,128)(2,1)}, u32[]{:S(2)}) copy-start(bf16[16,128,256]{2,1,0:T(8,128)(2,1)} %get-tuple-element.28.field_ref) | copy-start | bytes 3145732
  3.7 106.0 %copy-start.14 = (bf16[64,64]{1,0:T(8,128)(2,1)S(1)}, bf16[64,64]{1,0:T(8,128)(2,1)}, u32[]{:S(2)}) copy-start(bf16[64,64]{1,0:T(8,128)(2,1)} %param.15) | copy-start | bytes 24580
  36.7 17.8 %all-to-all-start.1 = ((bf16[8,32,1024]{2,1,0:T(8,128)(2,1)}), bf16[8,32,1024]{2,1,0:T(8,128)(2,1)S(1)}, u32[]{:S(2)}, u32[]{:S(2)}) async-start(bf16[8,32,1024]{2,1,0:T(8,128)(2,1)} %bitcast.30), calls=%async_computation.1 | async-start | bytes 1048576 | tf_op jit(solution)/shard_map/all_to_all | solution.py:440
  40.3 5.4 %collective-permute-start = (bf16[1024,128]{1,0:T(8,128)(2,1)}, bf16[1024,128]{1,0:T(8,128)(2,1)S(1)}, u32[]{:S(2)}, u32[]{:S(2)}) collective-permute-start(bf16[1024,128]{1,0:T(8,128)(2,1)} %get-tuple-element.32.refs_0_), channel_id=1, source_target_pairs={{0,8},{8,0},{16,24},{24,16},{1,9},{9,1},{17,25},{25,17},{2,10},{10... | collective-permute-start | bytes 786440 | tf_op jit(solution)/shard_map/ppermute | solution.py:392
  40.3 9.4 %collective-permute-start.1 = (bf16[1024,128]{1,0:T(8,128)(2,1)}, bf16[1024,128]{1,0:T(8,128)(2,1)S(1)}, u32[]{:S(2)}, u32[]{:S(2)}) collective-permute-start(bf16[1024,128]{1,0:T(8,128)(2,1)} %get-tuple-element.32.refs_0_), channel_id=1, source_target_pairs={{0,16},{8,24},{16,0},{24,8},{1,17},{9,25},{17,1},{25,9},{2,18},{10... | collective-permute-start | bytes 786440 | tf_op jit(solution)/shard_map/ppermute | solution.py:392
  41.9 12.5 %collective-permute-start.2 = (bf16[1024,128]{1,0:T(8,128)(2,1)}, bf16[1024,128]{1,0:T(8,128)(2,1)S(1)}, u32[]{:S(2)}, u32[]{:S(2)}) collective-permute-start(bf16[1024,128]{1,0:T(8,128)(2,1)} %get-tuple-element.32.refs_0_), channel_id=1, source_target_pairs={{0,24},{8,16},{16,8},{24,0},{1,25},{9,17},{17,9},{25,1},{2,26},{10... | collective-permute-start | bytes 786440 | tf_op jit(solution)/shard_map/ppermute | solution.py:392
  45.7 64.0 %copy-start.11 = (bf16[1024,128]{1,0:T(8,128)(2,1)}, bf16[1024,128]{1,0:T(8,128)(2,1)S(1)}, u32[]{:S(2)}) copy-start(bf16[1024,128]{1,0:T(8,128)(2,1)S(1)} %collective-permute-done.refs_1_) | copy-start | bytes 786436
  49.7 4.8 %copy-start.12 = (bf16[1024,128]{1,0:T(8,128)(2,1)}, bf16[1024,128]{1,0:T(8,128)(2,1)S(1)}, u32[]{:S(2)}) copy-start(bf16[1024,128]{1,0:T(8,128)(2,1)S(1)} %collective-permute-done.1.refs_2_) | copy-start | bytes 786436
  54.4 0.7 copy-start.13
  55.1 1.2 copy-start.1
  63.0 27.7 %all-to-all-start.2 = ((bf16[8,16,2048]{2,1,0:T(8,128)(2,1)}), bf16[8,16,2048]{2,1,0:T(8,128)(2,1)S(1)}, u32[]{:S(2)}, u32[]{:S(2)}) async-start(bf16[8,16,2048]{2,1,0:T(8,128)(2,1)} %bitcast.8), calls=%async_computation.2 | async-start | bytes 1048576 | tf_op jit(solution)/shard_map/all_to_all | solution.py:440
  69.0 14.4 %collective-permute-start.5 = (f32[64,64]{1,0:T(8,128)S(1)}, f32[64,64]{1,0:T(8,128)S(1)}, u32[]{:S(2)}, u32[]{:S(2)}) collective-permute-start(f32[64,64]{1,0:T(8,128)S(1)} %get-tuple-element.30), channel_id=1, source_target_pairs={{0,6},{1,7},{2,4},{3,5},{4,2},{5,3},{6,0},{7,1},{8,14},{9,15},{10,... | collective-permute-start | bytes 49160 | tf_op jit(solution)/shard_map/ppermute | solution.py:402
  72.8 13.8 %collective-permute-start.4 = (f32[64,64]{1,0:T(8,128)S(1)}, f32[64,64]{1,0:T(8,128)S(1)}, u32[]{:S(2)}, u32[]{:S(2)}) collective-permute-start(f32[64,64]{1,0:T(8,128)S(1)} %get-tuple-element.30), channel_id=1, source_target_pairs={{0,4},{1,5},{2,6},{3,7},{4,0},{5,1},{6,2},{7,3},{8,12},{9,13},{10,... | collective-permute-start | bytes 49160 | tf_op jit(solution)/shard_map/ppermute | solution.py:402
  72.8 13.8 %collective-permute-start.3 = (f32[64,64]{1,0:T(8,128)S(1)}, f32[64,64]{1,0:T(8,128)S(1)}, u32[]{:S(2)}, u32[]{:S(2)}) collective-permute-start(f32[64,64]{1,0:T(8,128)S(1)} %get-tuple-element.30), channel_id=1, source_target_pairs={{0,2},{1,3},{2,0},{3,1},{4,6},{5,7},{6,4},{7,5},{8,10},{9,11},{10,... | collective-permute-start | bytes 49160 | tf_op jit(solution)/shard_map/ppermute | solution.py:402
  86.7 4.0 %collective-permute-start.6 = (f32[64,64]{1,0:T(8,128)S(1)}, f32[64,64]{1,0:T(8,128)S(1)}, u32[]{:S(2)}, u32[]{:S(2)}) collective-permute-start(f32[64,64]{1,0:T(8,128)S(1)} %add_add_fusion), channel_id=1, source_target_pairs={{0,1},{1,0},{2,3},{3,2},{4,5},{5,4},{6,7},{7,6},{8,9},{9,8},{10,11... | collective-permute-start | bytes 49160 | tf_op jit(solution)/shard_map/ppermute | solution.py:402
  91.3 2.0 %copy-start = (bf16[1088,128]{1,0:T(8,128)(2,1)}, bf16[1088,128]{1,0:T(8,128)(2,1)S(1)}, u32[]{:S(2)}) copy-start(bf16[1088,128]{1,0:T(8,128)(2,1)S(1)} %grad_spectra.1.spec_ref.refs_4_.refs_8_) | copy-start | bytes 835588
  91.3 12.6 %collective-permute-start.7 = (bf16[1088,128]{1,0:T(8,128)(2,1)S(1)}, bf16[1088,128]{1,0:T(8,128)(2,1)S(1)}, u32[]{:S(2)}, u32[]{:S(2)}) collective-permute-start(bf16[1088,128]{1,0:T(8,128)(2,1)S(1)} %grad_spectra.1.spec_ref.refs_4_.refs_8_), channel_id=1, source_target_pairs={{0,8},{8,0},{16,24},{24,16},{1,9},{9,1},{17,25},{25,17},{2,10},{10... | collective-permute-start | bytes 835592 | tf_op jit(solution)/shard_map/ppermute | solution.py:392
  91.4 12.5 %collective-permute-start.8 = (bf16[1088,128]{1,0:T(8,128)(2,1)S(1)}, bf16[1088,128]{1,0:T(8,128)(2,1)S(1)}, u32[]{:S(2)}, u32[]{:S(2)}) collective-permute-start(bf16[1088,128]{1,0:T(8,128)(2,1)S(1)} %grad_spectra.1.spec_ref.refs_4_.refs_8_), channel_id=1, source_target_pairs={{0,16},{8,24},{16,0},{24,8},{1,17},{9,25},{17,1},{25,9},{2,18},{10... | collective-permute-start | bytes 835592 | tf_op jit(solution)/shard_map/ppermute | solution.py:392
  93.0 13.0 %collective-permute-start.9 = (bf16[1088,128]{1,0:T(8,128)(2,1)S(1)}, bf16[1088,128]{1,0:T(8,128)(2,1)S(1)}, u32[]{:S(2)}, u32[]{:S(2)}) collective-permute-start(bf16[1088,128]{1,0:T(8,128)(2,1)S(1)} %grad_spectra.1.spec_ref.refs_4_.refs_8_), channel_id=1, source_target_pairs={{0,24},{8,16},{16,8},{24,0},{1,25},{9,17},{17,9},{25,1},{2,26},{10... | collective-permute-start | bytes 835592 | tf_op jit(solution)/shard_map/ppermute | solution.py:392
  103.9 5.8 %copy-start.8 = (bf16[1088,128]{1,0:T(8,128)(2,1)}, bf16[1088,128]{1,0:T(8,128)(2,1)S(1)}, u32[]{:S(2)}) copy-start(bf16[1088,128]{1,0:T(8,128)(2,1)S(1)} %collective-permute-done.7.refs_5_.refs_9_) | copy-start | bytes 835588
  103.9 5.8 %copy-start.9 = (bf16[1088,128]{1,0:T(8,128)(2,1)}, bf16[1088,128]{1,0:T(8,128)(2,1)S(1)}, u32[]{:S(2)}) copy-start(bf16[1088,128]{1,0:T(8,128)(2,1)S(1)} %collective-permute-done.8.refs_6_.refs_10_) | copy-start | bytes 835588
  106.0 3.7 %copy-start.10 = (bf16[1088,128]{1,0:T(8,128)(2,1)}, bf16[1088,128]{1,0:T(8,128)(2,1)S(1)}, u32[]{:S(2)}) copy-start(bf16[1088,128]{1,0:T(8,128)(2,1)S(1)} %collective-permute-done.9.refs_7_.refs_11_) | copy-start | bytes 835588
  106.0 20.7 %all-to-all-start.3 = ((bf16[8,32,1024]{2,1,0:T(8,128)(2,1)}), bf16[8,32,1024]{2,1,0:T(8,128)(2,1)S(1)}, u32[]{:S(2)}, u32[]{:S(2)}) async-start(bf16[8,32,1024]{2,1,0:T(8,128)(2,1)} %bitcast.27), calls=%async_computation.3 | async-start | bytes 1048576 | tf_op jit(solution)/shard_map/all_to_all | solution.py:440
where the time goes:
time: 130 us; the launch traced here: 129 us
  Pallas kernels  53.8 us (41%)
  waiting for transfers between devices  26.5 us (20%)
  starting transfers between devices  23 us (18%)
  blocking collectives  22 us (17%)
  local copies, waits for them, and re-layouts  2.73 us (2%)
    pallas_call x8, Pallas kernels, call(): pl.pallas_call(kernel, out_shape=tuple(outs), grid=grid, in_specs=in_spec...  53.8 us
    all_to_all x1, blocking collectives, exchange(): lax.all_to_all(split, 'tile', split_axis=0, concat_axis=0, tiled=False)  22 us
    ppermute x4, waiting for transfers between devices, sum_over(): lax.ppermute(values, axis, [(i, i ^ step) for i in range(size)])  15.7 us
    all_to_all x3, starting transfers between devices, exchange(): lax.all_to_all(split, 'tile', split_axis=0, concat_axis=0, tiled=False)  13.3 us
    ppermute x6, waiting for transfers between devices, gather(): lax.ppermute(values, axis, [(i, i ^ step) for i in range(size)])  10.7 us
    ppermute x4, starting transfers between devices, sum_over(): lax.ppermute(values, axis, [(i, i ^ step) for i in range(size)])  5.94 us
    ppermute x6, starting transfers between devices, gather(): lax.ppermute(values, axis, [(i, i ^ step) for i in range(size)])  3.82 us
    unnamed x31, local copies, waits for them, and re-layouts  2.73 us
  transfers between devices with their start and end apart: 13, of which 7 were waited for; matrix products, arithmetic and copies ran while one was open for 1% of the time, Pallas kernels for 23%

commit v1 on v0

--- a/solution.py
+++ b/solution.py
@@ -130,10 +130,10 @@
     )
 
 
-def spectra_into(scale, owned, recv_ref, order_ref, rows_ref, spec_ref):
+def spectra_into(scale, owned, lanes, recv_ref, order_ref, rows_ref, spec_ref):
     count = order_ref.shape[0] // owned
-    lanes = recv_ref.shape[1] * count // rows_ref.shape[0]
-    ordered = [shuffle(order_ref, recv_ref[...])]
+    fields = rows_ref.shape[0] // count * lanes
+    ordered = [shuffle(order_ref, recv_ref[:, :fields])]
     for q in range(owned):
         stacked = stack(ordered, q, count, lanes)
         spec_ref[q * lanes : (q + 1) * lanes, :] = (
@@ -141,12 +141,23 @@
         ).astype(BF16)
 
 
-def grad_spectra_kernel(scale, owned, recv_ref, order_ref, rows_ref, local_ref, spec_ref):
-    spectra_into(scale, owned, recv_ref, order_ref, rows_ref, spec_ref)
-    value = local_ref[...]
+def to_piece(value):
+    return jnp.concatenate([value[n : n + PACK] for n in range(0, value.shape[0], PACK)], axis=1)
+
+
+def from_piece(value, extent):
+    return jnp.concatenate([value[:, n : n + extent] for n in range(0, value.shape[1], extent)], axis=0)
+
+
+def grad_spectra_kernel(scale, owned, lanes, channels, recv_ref, order_ref, rows_ref, spec_ref):
+    spectra_into(scale, owned, lanes, recv_ref, order_ref, rows_ref, spec_ref)
+    rows, width = recv_ref.shape
+    first = width - channels * channels // PACK
+    total = sum(recv_ref[n : n + PACK, first:].astype(F32) for n in range(0, rows, PACK))
+    value = from_piece(total, channels)
     high = value.astype(BF16)
     low = (value - high.astype(F32)).astype(BF16)
-    spec_ref[spec_ref.shape[0] - value.shape[0] :, :] = jnp.concatenate([high, low], axis=1)
+    spec_ref[spec_ref.shape[0] - channels :, :] = jnp.concatenate([high, low], axis=1)
 
 
 def tree(terms):
@@ -184,19 +195,19 @@
 def forward_kernel(scale, samples, owned, recv_ref, order_ref, rows_ref, back_ref, weight_ref, *rest):
     spec_ref, send_ref, real, imag, sums = rest
     _, _, outs, both = sums.shape
-    channels = weight_ref.shape[0] // outs
+    channels = weight_ref.shape[0] // outs // owned
     half = both // 2
     lanes = samples * channels
     q = pl.program_id(0)
 
     @pl.when(q == 0)
     def _():
-        spectra_into(scale, owned, recv_ref, order_ref, rows_ref, spec_ref)
+        spectra_into(scale, owned, lanes, recv_ref, order_ref, rows_ref, spec_ref)
         real[...], imag[...] = duplicates(spec_ref[...], half)
         sums[...] = jnp.zeros_like(sums)
 
     def body(block, carry):
-        view = rows_of(weight_ref, block, GROUP * outs)
+        view = rows_of(weight_ref, q * (channels // GROUP) + block, GROUP * outs)
         rows = []
         for s in range(samples):
             for store in (real, imag):
@@ -229,7 +240,7 @@
 
 def backward_kernel(samples, spec_ref, back_ref, weight_ref, send_ref, real, imag, sums):
     channels, both = sums.shape[2] // ROWS, sums.shape[3]
-    outs = weight_ref.shape[0] // channels
+    outs = weight_ref.shape[0] // channels // sums.shape[0]
     half = both // 2
     lanes = samples * outs
     q = pl.program_id(0)
@@ -246,7 +257,7 @@
     ]
 
     def body(block, carry):
-        view = rows_of(weight_ref, block, GROUP * outs)
+        view = rows_of(weight_ref, q * (channels // GROUP) + block, GROUP * outs)
         totals = []
         for step in range(GROUP):
             column = [view[step * outs + o : step * outs + o + PACK, :] for o in range(0, outs, PACK)]
@@ -273,8 +284,8 @@
     finish(back_ref, sums, send_ref, mix)
 
 
-def pixels_kernel(scale, heights, recv_ref, order_ref, back_ref, local_ref, field_ref, cot_ref, table_ref, *rest):
-    grad_ref, send_ref, sum_ref, ordered, total = rest
+def pixels_kernel(scale, heights, samples, recv_ref, order_ref, back_ref, local_ref, field_ref, cot_ref, table_ref, *rest):
+    grad_ref, send_ref, ordered, total = rest
     steps, lanes, _ = field_ref.shape
     count = order_ref.shape[0] // heights
     size = order_ref.shape[0]
@@ -297,14 +308,18 @@
         pre = pre + dot(local_ref[...], field_ref[step], ((1,), (0,)))
         grad = (cot_ref[step].astype(F32) * gelu_slope(pre)).astype(BF16)
         grad_ref[step] = grad
-        send_ref[:, step * lanes : (step + 1) * lanes] = dot(table_ref[...], grad, ((1,), (1,))).astype(BF16)
+        column = pl.ds(pl.multiple_of((group * steps + step) * lanes, lanes), lanes)
+        send_ref[:, column] = dot(table_ref[...], grad, ((1,), (1,))).astype(BF16)
         local = local + dot(field_ref[step], grad, ((1,), (1,)))
     total[...] += local
 
     @pl.when(group == pl.num_programs(0) - 1)
     def _():
-        extent = sum_ref.shape[0]
-        sum_ref[...] = sum(total[n : n + extent, n : n + extent] for n in range(0, lanes, extent))
+        extent = lanes // samples
+        partial = sum(total[n : n + extent, n : n + extent] for n in range(0, lanes, extent))
+        partial = to_piece(partial.astype(BF16))
+        for n in range(0, send_ref.shape[0], PACK):
+            send_ref[n : n + PACK, heights * lanes :] = partial
 
 
 def final_kernel(scale, recv_ref, order_ref, back_ref, local_ref, grad_ref, restore_ref, out_ref, result):
@@ -366,6 +381,9 @@
     lax.fori_loop(0, channels // GROUP, body, 0)
 
 
+IN_VMEM = pl.BlockSpec(memory_space=pltpu.VMEM)
+
+
 def whole(extent):
     return pl.BlockSpec(extent, lambda *_: (0,) * len(extent))
 
@@ -393,19 +411,6 @@
     ]
 
 
-def sum_over(values, axis):
-    size = lax.axis_size(axis)
-    top = size
-    while top > 1:
-        low = max(top // 4, 1)
-        values = sum(
-            (lax.ppermute(values, axis, [(i, i ^ step) for i in range(size)]) for step in range(low, top, low)),
-            values,
-        )
-        top = low
-    return values
-
-
 def block_diagonal(matrix, copies):
     zero = jnp.zeros_like(matrix)
     return jnp.concatenate(
@@ -481,30 +486,30 @@
             pltpu.VMEM((owned, 2 * samples, channels, both), F32),
         ],
         grid=(owned,),
-        blocks={4: weight_block},
+        blocks={4: IN_VMEM},
+        limit=SMALL,
     )
     all_spectra = gather(spectra, "dp")
     arrived = exchange(send)
     arrived, *all_spectra = lax.optimization_barrier((arrived, *all_spectra))
     steps = 4
     row_block = pl.BlockSpec((steps, lanes, width), lambda n: (n, 0, 0))
-    gate_rows, send, local_sum = call(
-        functools.partial(pixels_kernel, mode_scale, th),
+    gate_rows, send = call(
+        functools.partial(pixels_kernel, mode_scale, th, samples),
         "pixels",
         (arrived, by_height, back_cols, forward_mix, field_rows, cot_rows, send_cols),
-        (field_shape, to_modes, shape((channels, channels), F32)),
+        (field_shape, shape((halves, th * lanes + channels * channels // PACK))),
         [pltpu.VMEM((inverse, owned * lanes), BF16), pltpu.VMEM((lanes, lanes), F32)],
         grid=(th // steps,),
         blocks={4: row_block, 5: row_block},
-        out_blocks={0: row_block, 1: pl.BlockSpec((halves, steps * lanes), lambda n: (0, n))},
+        out_blocks={0: row_block},
         limit=SMALL,
     )
     arrived = exchange(send)
-    local_sum = sum_over(local_sum, "tile")
     (grad_spectra,) = call(
-        functools.partial(grad_spectra_kernel, mode_scale, owned),
+        functools.partial(grad_spectra_kernel, mode_scale, owned, lanes, channels),
         "grad_spectra",
-        (arrived, by_mode, rows, local_sum),
+        (arrived, by_mode, rows),
         (shape((owned * lanes + channels, both)),),
         limit=SMALL,
     )
@@ -520,7 +525,8 @@
             pltpu.VMEM((owned, 2 * samples, channels * ROWS, both), F32),
         ],
         grid=(owned,),
-        blocks={2: weight_block},
+        blocks={2: IN_VMEM},
+        limit=SMALL,
     )
     send, *all_grads = lax.optimization_barrier((send, *all_grads))
     arrived = exchange(send)

time: 130 us -> 127 us (0.977)
  blocking collectives: 22 us -> 44.6 us
  waiting for transfers between devices: 26.5 us -> 10.6 us
  starting transfers between devices: 23 us -> 10.9 us
  local copies, waits for them, and re-layouts: 2.73 us -> 11.7 us
  Pallas kernels: 53.8 us -> 46.9 us
    all_to_all x1 -> x2, blocking collectives: 22 us -> 44.6 us  [exchange(): lax.all_to_all(split, 'tile', split_axis=0, concat_axis=0, tiled=False)]
    ppermute x4 -> x0, waiting for transfers between devices: 15.7 us -> none  [sum_over(): lax.ppermute(values, axis, [(i, i ^ step) for i in range(size)])]
    unnamed x31 -> x45, local copies, waits for them, and re-layouts: 2.73 us -> 11.7 us
    pallas_call x8, Pallas kernels: 53.8 us -> 46.9 us  [call(): pl.pallas_call(kernel, out_shape=tuple(outs), grid=grid, in_specs=in_spec...]
    all_to_all x3 -> x2, starting transfers between devices: 13.3 us -> 7.09 us  [exchange(): lax.all_to_all(split, 'tile', split_axis=0, concat_axis=0, tiled=False)]
    ppermute x4 -> x0, starting transfers between devices: 5.94 us -> none  [sum_over(): lax.ppermute(values, axis, [(i, i ^ step) for i in range(size)])]
  transfers between devices with their start and end apart: 13 -> 8, of which waited for: 7 -> 4; matrix products, arithmetic and copies ran while one was open for 1% -> 1% of each run, Pallas kernels for 23% -> 22%
where the time goes in v1:
time: 127 us; the launch traced here: 126 us
  Pallas kernels  46.9 us (37%)
  blocking collectives  44.6 us (35%)
  local copies, waits for them, and re-layouts  11.7 us (9%)
  starting transfers between devices  10.9 us (9%)
  waiting for transfers between devices  10.6 us (8%)
    pallas_call x8, Pallas kernels, call(): pl.pallas_call(kernel, out_shape=tuple(outs), grid=grid, in_specs=in_spec...  46.9 us
    all_to_all x2, blocking collectives, exchange(): lax.all_to_all(split, 'tile', split_axis=0, concat_axis=0, tiled=False)  44.6 us
    unnamed x45, local copies, waits for them, and re-layouts  11.7 us
    ppermute x6, waiting for transfers between devices, gather(): lax.ppermute(values, axis, [(i, i ^ step) for i in range(size)])  10.3 us
    all_to_all x2, starting transfers between devices, exchange(): lax.all_to_all(split, 'tile', split_axis=0, concat_axis=0, tiled=False)  7.09 us
    ppermute x6, starting transfers between devices, gather(): lax.ppermute(values, axis, [(i, i ^ step) for i in range(size)])  3.82 us
  transfers between devices with their start and end apart: 8, of which 4 were waited for; matrix products, arithmetic and copies ran while one was open for 1% of the time, Pallas kernels for 22%

profile of v1, /device:TPU:0, one launch (start us, length us, event | category | flops | bytes accessed | tf_op | source)
XLA Modules:
  0.0 125.7 jit_solution(7526344910422315988)
XLA Ops:
  0.6 0.0 copy-start.4
  0.6 0.0 copy-start.8
  0.7 0.0 copy-start.14
  0.7 0.0 copy-start.10
  0.7 0.0 copy-start.7
  0.7 0.0 copy-start.12
  0.7 0.0 copy-start.21
  0.7 3.0 %columns.1 = (bf16[16,128,256]{2,1,0:T(8,128)(2,1)}, bf16[128,2048]{1,0:T(8,128)(2,1)}) custom-call(bf16[256,256]{1,0:T(8,128)(2,1)} %constant.30.order_ref.restore_ref, bf16[128,256]{1,0:T(8,128)(2,1)} %constant.31.table_ref, bf16[2048,256]{1,0:T(8,128)(2,1)} %bitcast.21, bf16[2048,256]{1,0:T(8,128)(2,1)} %bitcast.22, bf16[2048,256]{1,0:T(8,128)(2,1)} %bitcast.23, ...), custom_call_target="tpu_custom_call" | custom-call | tf_op jit(solution)/shard_map/columns/pallas_call | solution.py:395
  3.7 21.9 %all_to_all.20 = bf16[8,16,2048]{2,1,0:T(8,128)(2,1)S(1)} all-to-all(bf16[8,16,2048]{2,1,0:T(8,128)(2,1)} %bitcast.30), channel_id=1, replica_groups=mesh['dp'=4,'tile'=8] {'tile'}, dimensions={0} | all-to-all | bytes 1048576 | tf_op jit(solution)/shard_map/all_to_all | solution.py:445
  25.6 3.4 %copy-done = bf16[8,64,64,128]{3,2,1,0:T(8,128)(2,1)S(1)} copy-done((bf16[8,64,64,128]{3,2,1,0:T(8,128)(2,1)S(1)}, bf16[8,64,64,128]{3,2,1,0:T(8,128)(2,1)}, u32[]{:S(2)}) %copy-start) | copy-done | bytes 8388632
  29.0 0.8 copy-done.6
  29.8 0.8 copy-done.9
  30.7 0.8 copy-done.13
  31.4 7.9 %mix_forward.1 = (bf16[1024,128]{1,0:T(8,128)(2,1)S(1)}, bf16[256,1024]{1,0:T(8,128)(2,1)}) custom-call(bf16[128,2048]{1,0:T(8,128)(2,1)S(1)} %bitcast.17, bf16[128,128]{1,0:T(8,128)(2,1)S(1)} %copy-done.13, bf16[256,128]{1,0:T(8,128)(2,1)S(1)} %copy-done.9, bf16[256,128]{1,0:T(8,128)(2,1)S(1)} %copy-done.6, bf16[32768,128]{1,0:T(8,128)(2,1)S(1)} %bitcast.14), custom_call_target="tpu_custom_call" | custom-call | tf_op jit(solution)/shard_map/mix_forward/pallas_call | solution.py:395
  39.3 3.6 %all-to-all-start.1 = ((bf16[8,32,1024]{2,1,0:T(8,128)(2,1)}), bf16[8,32,1024]{2,1,0:T(8,128)(2,1)S(1)}, u32[]{:S(2)}, u32[]{:S(2)}) async-start(bf16[8,32,1024]{2,1,0:T(8,128)(2,1)} %bitcast.4), calls=%async_computation.1 | async-start | bytes 1048576 | tf_op jit(solution)/shard_map/all_to_all | solution.py:445
  42.9 0.0 collective-permute-start
  42.9 1.6 %collective-permute-start.1 = (bf16[1024,128]{1,0:T(8,128)(2,1)S(1)}, bf16[1024,128]{1,0:T(8,128)(2,1)S(1)}, u32[]{:S(2)}, u32[]{:S(2)}) collective-permute-start(bf16[1024,128]{1,0:T(8,128)(2,1)S(1)} %get-tuple-element.30.refs_0_), channel_id=1, source_target_pairs={{0,16},{8,24},{16,0},{24,8},{1,17},{9,25},{17,1},{25,9},{2,18},{10... | collective-permute-start | bytes 786440 | tf_op jit(solution)/shard_map/ppermute | solution.py:410
  44.5 0.3 collective-permute-start.2
  44.8 0.8 copy.15
  45.6 2.6 %relayout.1.cot_ref = bf16[16,128,256]{2,1,0:T(8,128)(2,1)} custom-call(bf16[256,256]{1,0:T(8,128)(2,1)} %constant.30.order_ref.restore_ref, bf16[2048,256]{1,0:T(8,128)(2,1)} %bitcast.25, bf16[2048,256]{1,0:T(8,128)(2,1)} %bitcast.26, bf16[2048,256]{1,0:T(8,128)(2,1)} %bitcast.27, bf16[2048,256]{1,0:T(8,128)(2,1)} %bitcast.28), custom_call_target="tpu_custom_call" | custom-call | tf_op jit(solution)/shard_map/relayout/pallas_call | solution.py:395
  48.2 0.1 fusion.4.local_ref
  48.3 0.0 collective-permute-done.refs_1_
  48.3 3.8 %collective-permute-done.1.refs_2_ = bf16[1024,128]{1,0:T(8,128)(2,1)S(1)} collective-permute-done((bf16[1024,128]{1,0:T(8,128)(2,1)S(1)}, bf16[1024,128]{1,0:T(8,128)(2,1)S(1)}, u32[]{:S(2)}, u32[]{:S(2)}) %collective-permute-start.1) | collective-permute-done | bytes 262176 | tf_op jit(solution)/shard_map/ppermute | solution.py:410
  52.1 4.7 %collective-permute-done.2.refs_3_ = bf16[1024,128]{1,0:T(8,128)(2,1)S(1)} collective-permute-done((bf16[1024,128]{1,0:T(8,128)(2,1)S(1)}, bf16[1024,128]{1,0:T(8,128)(2,1)S(1)}, u32[]{:S(2)}, u32[]{:S(2)}) %collective-permute-start.2) | collective-permute-done | bytes 262176 | tf_op jit(solution)/shard_map/ppermute | solution.py:410
  56.8 0.3 all-to-all-done.1
  57.0 0.0 copy-done.18
  57.1 0.0 copy-done.19
  57.1 0.4 copy-done.20
  57.5 0.0 copy-done.12
  57.5 0.0 copy-start.3
  57.5 1.2 copy-done.3
  58.7 6.0 %pixels.1 = (bf16[16,128,256]{2,1,0:T(8,128)(2,1)S(1)}, bf16[128,2304]{1,0:T(8,128)(2,1)S(1)}) custom-call(bf16[256,1024]{1,0:T(8,128)(2,1)S(1)} %bitcast.18, bf16[256,256]{1,0:T(8,128)(2,1)S(1)} %copy-done.4, bf16[128,256]{1,0:T(8,128)(2,1)S(1)} %copy-done.12, bf16[128,128]{1,0:T(8,128)(2,1)S(1)} %fusion.4.local_ref, bf16[16,128,256]{2,1,0:T(8,128)(2,1)S(1)} %copy-done.5, ...), custom_call_target="tpu_custom_call" | custom-call | tf_op jit(solution)/shard_map/pixels/pallas_call | solution.py:395
  64.8 22.7 %all_to_all.21 = bf16[8,16,2304]{2,1,0:T(8,128)(2,1)S(1)} all-to-all(bf16[8,16,2304]{2,1,0:T(8,128)(2,1)S(1)} %bitcast.20), channel_id=1, replica_groups=mesh['dp'=4,'tile'=8] {'tile'}, dimensions={0} | all-to-all | bytes 1179648 | tf_op jit(solution)/shard_map/all_to_all | solution.py:445
  87.5 0.6 grad_spectra.1.spec_ref.refs_4_.refs_8_
  88.1 0.1 collective-permute-start.3
  88.2 1.6 %collective-permute-start.4 = (bf16[1088,128]{1,0:T(8,128)(2,1)S(1)}, bf16[1088,128]{1,0:T(8,128)(2,1)S(1)}, u32[]{:S(2)}, u32[]{:S(2)}) collective-permute-start(bf16[1088,128]{1,0:T(8,128)(2,1)S(1)} %grad_spectra.1.spec_ref.refs_4_.refs_8_), channel_id=1, source_target_pairs={{0,16},{8,24},{16,0},{24,8},{1,17},{9,25},{17,1},{25,9},{2,18},{10... | collective-permute-start | bytes 835592 | tf_op jit(solution)/shard_map/ppermute | solution.py:410
  89.8 0.3 collective-permute-start.5
  90.1 3.4 %copy-done.1 = bf16[8,64,64,128]{3,2,1,0:T(8,128)(2,1)S(1)} copy-done((bf16[8,64,64,128]{3,2,1,0:T(8,128)(2,1)S(1)}, bf16[8,64,64,128]{3,2,1,0:T(8,128)(2,1)}, u32[]{:S(2)}) %copy-start.1) | copy-done | bytes 8388632
  93.4 7.5 %mix_backward.1 = bf16[256,1024]{1,0:T(8,128)(2,1)} custom-call(bf16[1088,128]{1,0:T(8,128)(2,1)S(1)} %grad_spectra.1.spec_ref.refs_4_.refs_8_, bf16[256,128]{1,0:T(8,128)(2,1)S(1)} %copy-done.7, bf16[32768,128]{1,0:T(8,128)(2,1)S(1)} %bitcast.15), custom_call_target="tpu_custom_call" | custom-call | tf_op jit(solution)/shard_map/mix_backward/pallas_call | solution.py:395
  100.9 0.0 collective-permute-done.3.refs_5_.refs_9_
  100.9 0.0 collective-permute-done.4.refs_6_.refs_10_
  101.0 1.8 %collective-permute-done.5.refs_7_.refs_11_ = bf16[1088,128]{1,0:T(8,128)(2,1)S(1)} collective-permute-done((bf16[1088,128]{1,0:T(8,128)(2,1)S(1)}, bf16[1088,128]{1,0:T(8,128)(2,1)S(1)}, u32[]{:S(2)}, u32[]{:S(2)}) %collective-permute-start.5) | collective-permute-done | bytes 278560 | tf_op jit(solution)/shard_map/ppermute | solution.py:410
  102.8 3.5 %all-to-all-start.3 = ((bf16[8,32,1024]{2,1,0:T(8,128)(2,1)}), bf16[8,32,1024]{2,1,0:T(8,128)(2,1)S(1)}, u32[]{:S(2)}, u32[]{:S(2)}) async-start(bf16[8,32,1024]{2,1,0:T(8,128)(2,1)} %bitcast.10), calls=%async_computation.3 | async-start | bytes 1048576 | tf_op jit(solution)/shard_map/all_to_all | solution.py:445
  106.3 0.0 copy-done.21
  106.3 0.1 fusion.5.local_ref
  106.4 17.0 %mode_grad.1 = (f32[32768,128]{1,0:T(8,128)}, f32[64,64]{1,0:T(8,128)}) custom-call(bf16[1024,128]{1,0:T(8,128)(2,1)} %copy-done.11, bf16[1024,128]{1,0:T(8,128)(2,1)} %copy-done.18, bf16[1024,128]{1,0:T(8,128)(2,1)} %copy-done.19, bf16[1024,128]{1,0:T(8,128)(2,1)} %copy-done.20, bf16[1088,128]{1,0:T(8,128)(2,1)} %copy-done.2, bf16[1088,128]{1,0:T(8,128)(2,1)} %copy-done.15, ...), custom_call_target="tpu_custom_call" | custom-call | tf_op jit(solution)/shard_map/mode_grad/pallas_call | solution.py:395
  123.4 0.0 all-to-all-done.3
  123.4 2.3 %final.1 = bf16[2048,256]{1,0:T(8,128)(2,1)} custom-call(bf16[256,1024]{1,0:T(8,128)(2,1)S(1)} %bitcast.19, bf16[256,256]{1,0:T(8,128)(2,1)S(1)} %copy-done.4, bf16[128,256]{1,0:T(8,128)(2,1)S(1)} %copy-done.12, bf16[128,128]{1,0:T(8,128)(2,1)S(1)} %fusion.5.local_ref, bf16[16,128,256]{2,1,0:T(8,128)(2,1)S(1)} %get-tuple-element.40.grad_ref, ...), custom_call_target="tpu_custom_call" | custom-call | tf_op jit(solution)/shard_map/final/pallas_call | solution.py:395
  (25 shorter events, 0.0 us)
Async XLA Ops:
  0.6 56.9 %copy-start.4 = (bf16[256,256]{1,0:T(8,128)(2,1)S(1)}, bf16[256,256]{1,0:T(8,128)(2,1)}, u32[]{:S(2)}) copy-start(bf16[256,256]{1,0:T(8,128)(2,1)} %constant.30.order_ref.restore_ref) | copy-start | bytes 393220
  0.6 56.9 %copy-start.8 = (bf16[128,256]{1,0:T(8,128)(2,1)S(1)}, bf16[128,256]{1,0:T(8,128)(2,1)}, u32[]{:S(2)}) copy-start(bf16[128,256]{1,0:T(8,128)(2,1)} %constant.31.table_ref) | copy-start | bytes 196612
  0.7 86.8 %copy-start.14 = (bf16[128,128]{1,0:T(8,128)(2,1)S(1)}, bf16[128,128]{1,0:T(8,128)(2,1)}, u32[]{:S(2)}) copy-start(bf16[128,128]{1,0:T(8,128)(2,1)} %constant.32.order_ref) | copy-start | bytes 98308
  0.7 86.8 %copy-start.10 = (bf16[256,128]{1,0:T(8,128)(2,1)S(1)}, bf16[256,128]{1,0:T(8,128)(2,1)}, u32[]{:S(2)}) copy-start(bf16[256,128]{1,0:T(8,128)(2,1)} %constant.33.rows_ref) | copy-start | bytes 196612
  0.7 89.4 %copy-start.7 = (bf16[256,128]{1,0:T(8,128)(2,1)S(1)}, bf16[256,128]{1,0:T(8,128)(2,1)}, u32[]{:S(2)}) copy-start(bf16[256,128]{1,0:T(8,128)(2,1)} %constant.34.back_ref) | copy-start | bytes 196612
  0.7 56.8 %copy-start.12 = (bf16[128,256]{1,0:T(8,128)(2,1)S(1)}, bf16[128,256]{1,0:T(8,128)(2,1)}, u32[]{:S(2)}) copy-start(bf16[128,256]{1,0:T(8,128)(2,1)} %constant.35.back_ref) | copy-start | bytes 196612
  0.7 105.6 %copy-start.21 = (bf16[64,64]{1,0:T(8,128)(2,1)S(1)}, bf16[64,64]{1,0:T(8,128)(2,1)}, u32[]{:S(2)}) copy-start(bf16[64,64]{1,0:T(8,128)(2,1)} %param.15) | copy-start | bytes 24580
  3.7 53.8 %copy-start.5 = (bf16[16,128,256]{2,1,0:T(8,128)(2,1)S(1)}, bf16[16,128,256]{2,1,0:T(8,128)(2,1)}, u32[]{:S(2)}) copy-start(bf16[16,128,256]{2,1,0:T(8,128)(2,1)} %get-tuple-element.27.field_ref) | copy-start | bytes 3145732
  25.6 3.4 %copy-start = (bf16[8,64,64,128]{3,2,1,0:T(8,128)(2,1)S(1)}, bf16[8,64,64,128]{3,2,1,0:T(8,128)(2,1)}, u32[]{:S(2)}) copy-start(bf16[8,64,64,128]{3,2,1,0:T(8,128)(2,1)} %param.14) | copy-start | bytes 25165828
  29.0 0.8 copy-start.6
  29.8 0.8 copy-start.9
  30.7 0.8 copy-start.13
  39.3 67.1 %copy-start.11 = (bf16[1024,128]{1,0:T(8,128)(2,1)}, bf16[1024,128]{1,0:T(8,128)(2,1)S(1)}, u32[]{:S(2)}) copy-start(bf16[1024,128]{1,0:T(8,128)(2,1)S(1)} %get-tuple-element.30.refs_0_) | copy-start | bytes 786436
  39.3 17.8 %all-to-all-start.1 = ((bf16[8,32,1024]{2,1,0:T(8,128)(2,1)}), bf16[8,32,1024]{2,1,0:T(8,128)(2,1)S(1)}, u32[]{:S(2)}, u32[]{:S(2)}) async-start(bf16[8,32,1024]{2,1,0:T(8,128)(2,1)} %bitcast.4), calls=%async_computation.1 | async-start | bytes 1048576 | tf_op jit(solution)/shard_map/all_to_all | solution.py:445
  42.9 5.4 %collective-permute-start = (bf16[1024,128]{1,0:T(8,128)(2,1)S(1)}, bf16[1024,128]{1,0:T(8,128)(2,1)S(1)}, u32[]{:S(2)}, u32[]{:S(2)}) collective-permute-start(bf16[1024,128]{1,0:T(8,128)(2,1)S(1)} %get-tuple-element.30.refs_0_), channel_id=1, source_target_pairs={{0,8},{8,0},{16,24},{24,16},{1,9},{9,1},{17,25},{25,17},{2,10},{10... | collective-permute-start | bytes 786440 | tf_op jit(solution)/shard_map/ppermute | solution.py:410
  42.9 9.2 %collective-permute-start.1 = (bf16[1024,128]{1,0:T(8,128)(2,1)S(1)}, bf16[1024,128]{1,0:T(8,128)(2,1)S(1)}, u32[]{:S(2)}, u32[]{:S(2)}) collective-permute-start(bf16[1024,128]{1,0:T(8,128)(2,1)S(1)} %get-tuple-element.30.refs_0_), channel_id=1, source_target_pairs={{0,16},{8,24},{16,0},{24,8},{1,17},{9,25},{17,1},{25,9},{2,18},{10... | collective-permute-start | bytes 786440 | tf_op jit(solution)/shard_map/ppermute | solution.py:410
  44.5 12.3 %collective-permute-start.2 = (bf16[1024,128]{1,0:T(8,128)(2,1)S(1)}, bf16[1024,128]{1,0:T(8,128)(2,1)S(1)}, u32[]{:S(2)}, u32[]{:S(2)}) collective-permute-start(bf16[1024,128]{1,0:T(8,128)(2,1)S(1)} %get-tuple-element.30.refs_0_), channel_id=1, source_target_pairs={{0,24},{8,16},{16,8},{24,0},{1,25},{9,17},{17,9},{25,1},{2,26},{10... | collective-permute-start | bytes 786440 | tf_op jit(solution)/shard_map/ppermute | solution.py:410
  48.3 8.8 %copy-start.18 = (bf16[1024,128]{1,0:T(8,128)(2,1)}, bf16[1024,128]{1,0:T(8,128)(2,1)S(1)}, u32[]{:S(2)}) copy-start(bf16[1024,128]{1,0:T(8,128)(2,1)S(1)} %collective-permute-done.refs_1_) | copy-start | bytes 786436
  52.1 5.0 %copy-start.19 = (bf16[1024,128]{1,0:T(8,128)(2,1)}, bf16[1024,128]{1,0:T(8,128)(2,1)S(1)}, u32[]{:S(2)}) copy-start(bf16[1024,128]{1,0:T(8,128)(2,1)S(1)} %collective-permute-done.1.refs_2_) | copy-start | bytes 786436
  56.8 0.7 copy-start.20
  57.5 1.2 copy-start.3
  88.1 18.3 %copy-start.2 = (bf16[1088,128]{1,0:T(8,128)(2,1)}, bf16[1088,128]{1,0:T(8,128)(2,1)S(1)}, u32[]{:S(2)}) copy-start(bf16[1088,128]{1,0:T(8,128)(2,1)S(1)} %grad_spectra.1.spec_ref.refs_4_.refs_8_) | copy-start | bytes 835588
  88.1 12.8 %collective-permute-start.3 = (bf16[1088,128]{1,0:T(8,128)(2,1)S(1)}, bf16[1088,128]{1,0:T(8,128)(2,1)S(1)}, u32[]{:S(2)}, u32[]{:S(2)}) collective-permute-start(bf16[1088,128]{1,0:T(8,128)(2,1)S(1)} %grad_spectra.1.spec_ref.refs_4_.refs_8_), channel_id=1, source_target_pairs={{0,8},{8,0},{16,24},{24,16},{1,9},{9,1},{17,25},{25,17},{2,10},{10... | collective-permute-start | bytes 835592 | tf_op jit(solution)/shard_map/ppermute | solution.py:410
  88.2 12.8 %collective-permute-start.4 = (bf16[1088,128]{1,0:T(8,128)(2,1)S(1)}, bf16[1088,128]{1,0:T(8,128)(2,1)S(1)}, u32[]{:S(2)}, u32[]{:S(2)}) collective-permute-start(bf16[1088,128]{1,0:T(8,128)(2,1)S(1)} %grad_spectra.1.spec_ref.refs_4_.refs_8_), channel_id=1, source_target_pairs={{0,16},{8,24},{16,0},{24,8},{1,17},{9,25},{17,1},{25,9},{2,18},{10... | collective-permute-start | bytes 835592 | tf_op jit(solution)/shard_map/ppermute | solution.py:410
  89.8 13.0 %collective-permute-start.5 = (bf16[1088,128]{1,0:T(8,128)(2,1)S(1)}, bf16[1088,128]{1,0:T(8,128)(2,1)S(1)}, u32[]{:S(2)}, u32[]{:S(2)}) collective-permute-start(bf16[1088,128]{1,0:T(8,128)(2,1)S(1)} %grad_spectra.1.spec_ref.refs_4_.refs_8_), channel_id=1, source_target_pairs={{0,24},{8,16},{16,8},{24,0},{1,25},{9,17},{17,9},{25,1},{2,26},{10... | collective-permute-start | bytes 835592 | tf_op jit(solution)/shard_map/ppermute | solution.py:410
  90.1 3.4 %copy-start.1 = (bf16[8,64,64,128]{3,2,1,0:T(8,128)(2,1)S(1)}, bf16[8,64,64,128]{3,2,1,0:T(8,128)(2,1)}, u32[]{:S(2)}) copy-start(bf16[8,64,64,128]{3,2,1,0:T(8,128)(2,1)} %param.14) | copy-start | bytes 25165828
  100.9 5.4 %copy-start.15 = (bf16[1088,128]{1,0:T(8,128)(2,1)}, bf16[1088,128]{1,0:T(8,128)(2,1)S(1)}, u32[]{:S(2)}) copy-start(bf16[1088,128]{1,0:T(8,128)(2,1)S(1)} %collective-permute-done.3.refs_5_.refs_9_) | copy-start | bytes 835588
  101.0 5.4 %copy-start.16 = (bf16[1088,128]{1,0:T(8,128)(2,1)}, bf16[1088,128]{1,0:T(8,128)(2,1)S(1)}, u32[]{:S(2)}) copy-start(bf16[1088,128]{1,0:T(8,128)(2,1)S(1)} %collective-permute-done.4.refs_6_.refs_10_) | copy-start | bytes 835588
  102.8 3.6 %copy-start.17 = (bf16[1088,128]{1,0:T(8,128)(2,1)}, bf16[1088,128]{1,0:T(8,128)(2,1)S(1)}, u32[]{:S(2)}) copy-start(bf16[1088,128]{1,0:T(8,128)(2,1)S(1)} %collective-permute-done.5.refs_7_.refs_11_) | copy-start | bytes 835588
  102.8 20.6 %all-to-all-start.3 = ((bf16[8,32,1024]{2,1,0:T(8,128)(2,1)}), bf16[8,32,1024]{2,1,0:T(8,128)(2,1)S(1)}, u32[]{:S(2)}, u32[]{:S(2)}) async-start(bf16[8,32,1024]{2,1,0:T(8,128)(2,1)} %bitcast.10), calls=%async_computation.3 | async-start | bytes 1048576 | tf_op jit(solution)/shard_map/all_to_all | solution.py:445

commit v2 on v0

--- a/solution.py
+++ b/solution.py
@@ -17,6 +17,7 @@
 PACK = 16
 GROUP = 8
 SPLIT = 4
+AHEAD = 3
 
 
 def row_tables(height, modes):
@@ -114,9 +115,9 @@
     by_rows(order_ref, rest[:SPLIT], rest[SPLIT])
 
 
-def shuffle_groups(order_ref, recv_ref):
+def shuffle_groups(order_ref, recv_ref, width):
     size = order_ref.shape[0]
-    return [shuffle(order_ref, recv_ref[n : n + size, :]) for n in range(0, recv_ref.shape[0], size)]
+    return [shuffle(order_ref, recv_ref[n : n + size, :width]) for n in range(0, recv_ref.shape[0], size)]
 
 
 def stack(groups, index, count, lanes):
@@ -130,10 +131,10 @@
     )
 
 
-def spectra_into(scale, owned, recv_ref, order_ref, rows_ref, spec_ref):
+def spectra_into(scale, owned, lanes, recv_ref, order_ref, rows_ref, spec_ref):
     count = order_ref.shape[0] // owned
-    lanes = recv_ref.shape[1] * count // rows_ref.shape[0]
-    ordered = [shuffle(order_ref, recv_ref[...])]
+    fields = rows_ref.shape[0] // count * lanes
+    ordered = [shuffle(order_ref, recv_ref[:, :fields])]
     for q in range(owned):
         stacked = stack(ordered, q, count, lanes)
         spec_ref[q * lanes : (q + 1) * lanes, :] = (
@@ -141,12 +142,16 @@
         ).astype(BF16)
 
 
-def grad_spectra_kernel(scale, owned, recv_ref, order_ref, rows_ref, local_ref, spec_ref):
-    spectra_into(scale, owned, recv_ref, order_ref, rows_ref, spec_ref)
-    value = local_ref[...]
-    high = value.astype(BF16)
-    low = (value - high.astype(F32)).astype(BF16)
-    spec_ref[spec_ref.shape[0] - value.shape[0] :, :] = jnp.concatenate([high, low], axis=1)
+def to_piece(value, rows):
+    return jnp.concatenate([value[n : n + rows] for n in range(0, value.shape[0], rows)], axis=1)
+
+
+def from_piece(value, extent):
+    return jnp.concatenate([value[:, n : n + extent] for n in range(0, value.shape[1], extent)], axis=0)
+
+
+def spectra_kernel(scale, owned, lanes, recv_ref, order_ref, rows_ref, spec_ref):
+    spectra_into(scale, owned, lanes, recv_ref, order_ref, rows_ref, spec_ref)
 
 
 def tree(terms):
@@ -175,25 +180,49 @@
     @pl.when(pl.program_id(0) == pl.num_programs(0) - 1)
     def _():
         owned = sums.shape[0]
-        lanes = send_ref.shape[1] // owned
         for q in range(owned):
             mixed = mix(sums.at[q]).astype(BF16)
+            lanes = mixed.shape[0]
             send_ref[:, q * lanes : (q + 1) * lanes] = dot(back_ref[...], mixed, ((1,), (1,))).astype(BF16)
 
 
-def forward_kernel(scale, samples, owned, recv_ref, order_ref, rows_ref, back_ref, weight_ref, *rest):
-    spec_ref, send_ref, real, imag, sums = rest
+def fetch_weights(source_ref, weights, sems):
+    q = pl.program_id(0)
+    owned = sems.shape[0]
+    size = weights.shape[0] // owned
+
+    def move(mode):
+        part = pl.ds(pl.multiple_of(mode * size, size), size)
+        return pltpu.make_async_copy(source_ref.at[part, :], weights.at[part, :], sems.at[mode])
+
+    @pl.when(q == 0)
+    def _():
+        for mode in range(min(AHEAD, owned)):
+            move(mode).start()
+
+    @pl.when(q + AHEAD < owned)
+    def _():
+        move(q + AHEAD).start()
+
+    return move(q), weights.at[pl.ds(pl.multiple_of(q * size, size), size), :]
+
+
+def forward_kernel(scale, samples, owned, recv_ref, order_ref, rows_ref, back_ref, source_ref, *rest):
+    spec_ref, send_ref, real, imag, sums, weights, sems = rest
     _, _, outs, both = sums.shape
-    channels = weight_ref.shape[0] // outs
+    channels = weights.shape[0] // outs // owned
     half = both // 2
     lanes = samples * channels
     q = pl.program_id(0)
+    coming, weight_ref = fetch_weights(source_ref, weights, sems)
 
     @pl.when(q == 0)
     def _():
-        spectra_into(scale, owned, recv_ref, order_ref, rows_ref, spec_ref)
+        spectra_into(scale, owned, lanes, recv_ref, order_ref, rows_ref, spec_ref)
         real[...], imag[...] = duplicates(spec_ref[...], half)
         sums[...] = jnp.zeros_like(sums)
+
+    coming.wait()
 
     def body(block, carry):
         view = rows_of(weight_ref, block, GROUP * outs)
@@ -227,18 +256,25 @@
     finish(back_ref, sums, send_ref, mix)
 
 
-def backward_kernel(samples, spec_ref, back_ref, weight_ref, send_ref, real, imag, sums):
+def backward_kernel(samples, tiles, spec_ref, back_ref, local_ref, source_ref, *rest):
+    send_ref, real, imag, sums, weights, sems = rest
     channels, both = sums.shape[2] // ROWS, sums.shape[3]
-    outs = weight_ref.shape[0] // channels
+    outs = weights.shape[0] // channels // sums.shape[0]
     half = both // 2
     lanes = samples * outs
     q = pl.program_id(0)
+    coming, weight_ref = fetch_weights(source_ref, weights, sems)
 
     @pl.when(q == 0)
     def _():
-        first, second = duplicates(spec_ref[: real.shape[0], :], half)
+        first, second = duplicates(spec_ref[...], half)
         real[...], imag[...] = first.astype(BF16), second.astype(BF16)
-
+        extent = send_ref.shape[0] // tiles
+        partial = to_piece(local_ref[...].astype(BF16), extent)
+        for n in range(0, send_ref.shape[0], extent):
+            send_ref[n : n + extent, sums.shape[0] * lanes :] = partial
+
+    coming.wait()
     grads = [
         [store[pl.ds(pl.multiple_of(q * lanes + s * outs + o, PACK), PACK), :] for o in range(0, outs, PACK)]
         for s in range(samples)
@@ -307,10 +343,15 @@
         sum_ref[...] = sum(total[n : n + extent, n : n + extent] for n in range(0, lanes, extent))
 
 
-def final_kernel(scale, recv_ref, order_ref, back_ref, local_ref, grad_ref, restore_ref, out_ref, result):
+def final_kernel(scale, tiles, recv_ref, order_ref, back_ref, local_ref, grad_ref, restore_ref, *rest):
+    out_ref, sum_ref, result = rest
     heights, lanes, _ = grad_ref.shape
+    extent = recv_ref.shape[0] // tiles
+    first = back_ref.shape[0] // (2 * tiles) * lanes
+    partials = sum(recv_ref[n : n + extent, first:].astype(F32) for n in range(0, recv_ref.shape[0], extent))
+    sum_ref[...] = from_piece(partials, sum_ref.shape[1])
     count = order_ref.shape[0] // heights
-    ordered = shuffle_groups(order_ref, recv_ref)
+    ordered = shuffle_groups(order_ref, recv_ref, first)
     for h in range(heights):
         inner = stack(ordered, h, count, lanes)
         value = scale * dot(inner, back_ref[...], ((0,), (0,)))
@@ -322,20 +363,12 @@
 
 
 def outer_kernel(samples, groups, *refs):
-    specs, grads, pairs = refs[:groups], refs[groups : 2 * groups], refs[2 * groups : 3 * groups]
-    out_ref, local_ref, real, imag, plain, crossed = refs[3 * groups :]
+    specs, grads = refs[:groups], refs[groups : 2 * groups]
+    out_ref, real, imag, plain, crossed = refs[2 * groups :]
     total, channels, both = real.shape
     outs = plain.shape[1]
     half = both // 2
     low = low_half((channels, both), half)
-
-    @pl.when(pl.program_id(0) == 0)
-    def _():
-        value = 0.0
-        for pair_ref in pairs:
-            pair = pair_ref[...].astype(F32)
-            value = value + pair[:, :channels] + pair[:, channels : 2 * channels]
-        local_ref[...] = value
 
     for g in range(groups):
         for s in range(samples):
@@ -386,23 +419,28 @@
     )(*operands)
 
 
-def gather(values, axis):
+def swap(values, axis, step):
+    return lax.ppermute(values, axis, [(i, i ^ step) for i in range(lax.axis_size(axis))])
+
+
+def gather_near(values, axis):
     size = lax.axis_size(axis)
-    return [values] + [
-        lax.ppermute(values, axis, [(i, i ^ step) for i in range(size)]) for step in range(1, size)
-    ]
+    return {0: values} | {1 << bit: swap(values, axis, 1 << bit) for bit in range(size.bit_length() - 1)}
+
+
+def gather_far(near, axis):
+    whole_set = dict(near)
+    for step in range(1, lax.axis_size(axis)):
+        if step not in whole_set:
+            whole_set[step] = swap(whole_set[step & (step - 1)], axis, step & -step)
+    return [whole_set[step] for step in sorted(whole_set)]
 
 
 def sum_over(values, axis):
-    size = lax.axis_size(axis)
-    top = size
-    while top > 1:
-        low = max(top // 4, 1)
-        values = sum(
-            (lax.ppermute(values, axis, [(i, i ^ step) for i in range(size)]) for step in range(low, top, low)),
-            values,
-        )
-        top = low
+    step = 1
+    while step < lax.axis_size(axis):
+        values = values + swap(values, axis, step)
+        step *= 2
     return values
 
 
@@ -448,6 +486,8 @@
     by_height = order(2 * min(tiles, 8), th)
     flat_weight = mode_weight.reshape(-1, both)
     weight_block = pl.BlockSpec((flat_weight.shape[0] // owned, both), lambda q: (q, 0))
+    weight_scratch = [pltpu.VMEM(flat_weight.shape, BF16), pltpu.SemaphoreType.DMA((owned,))]
+    in_place = pl.BlockSpec(memory_space=pl.ANY)
     to_modes = shape((halves, th * lanes))
     to_pixels = shape((inverse, owned * lanes))
     field_shape = shape((th, lanes, width))
@@ -479,13 +519,13 @@
             pltpu.VMEM((owned * lanes, both), F32),
             pltpu.VMEM((owned * lanes, both), F32),
             pltpu.VMEM((owned, 2 * samples, channels, both), F32),
+            *weight_scratch,
         ],
         grid=(owned,),
-        blocks={4: weight_block},
-    )
-    all_spectra = gather(spectra, "dp")
+        blocks={4: in_place},
+    )
+    all_spectra = gather_far(gather_near(spectra, "dp"), "dp")
     arrived = exchange(send)
-    arrived, *all_spectra = lax.optimization_barrier((arrived, *all_spectra))
     steps = 4
     row_block = pl.BlockSpec((steps, lanes, width), lambda n: (n, 0, 0))
     gate_rows, send, local_sum = call(
@@ -499,54 +539,55 @@
         out_blocks={0: row_block, 1: pl.BlockSpec((halves, steps * lanes), lambda n: (0, n))},
         limit=SMALL,
     )
+    send, *all_spectra = lax.optimization_barrier((send, *all_spectra))
     arrived = exchange(send)
-    local_sum = sum_over(local_sum, "tile")
+    local_sum = sum_over(local_sum, "dp")
     (grad_spectra,) = call(
-        functools.partial(grad_spectra_kernel, mode_scale, owned),
+        functools.partial(spectra_kernel, mode_scale, owned, lanes),
         "grad_spectra",
-        (arrived, by_mode, rows, local_sum),
-        (shape((owned * lanes + channels, both)),),
+        (arrived, by_mode, rows),
+        (shape((owned * lanes, both)),),
         limit=SMALL,
     )
-    all_grads = gather(grad_spectra, "dp")
+    near = gather_near(grad_spectra, "dp")
     (send,) = call(
-        functools.partial(backward_kernel, samples),
+        functools.partial(backward_kernel, samples, tiles),
         "mix_backward",
-        (grad_spectra, back_rows, flat_weight),
-        (to_pixels,),
+        (grad_spectra, back_rows, local_sum, flat_weight),
+        (shape((inverse, owned * lanes + channels * channels * tiles // inverse)),),
         [
             pltpu.VMEM((owned * lanes, both), BF16),
             pltpu.VMEM((owned * lanes, both), BF16),
             pltpu.VMEM((owned, 2 * samples, channels * ROWS, both), F32),
+            *weight_scratch,
         ],
         grid=(owned,),
-        blocks={2: weight_block},
-    )
-    send, *all_grads = lax.optimization_barrier((send, *all_grads))
+        blocks={3: in_place},
+    )
+    send, near = lax.optimization_barrier((send, near))
+    all_grads = gather_far(near, "dp")
     arrived = exchange(send)
 
     groups = lax.axis_size("dp")
     total = groups * samples
     per_mode = pl.BlockSpec((lanes, both), lambda q: (q, 0))
-    below = owned * lanes // channels
-    pair_block = pl.BlockSpec((channels, both), lambda q: (below, 0))
-    mode_grad, local_grad = call(
+    (mode_grad,) = call(
         functools.partial(outer_kernel, samples, groups),
         "mode_grad",
-        (*all_spectra, *all_grads, *all_grads),
-        (shape(flat_weight.shape, F32), shape((channels, channels), F32)),
+        (*all_spectra, *all_grads),
+        (shape(flat_weight.shape, F32),),
         [pltpu.VMEM((total, channels, both), F32)] * 2 + [pltpu.VMEM((total, channels, both), BF16)] * 2,
         grid=(owned,),
-        blocks={n: per_mode if n < 2 * groups else pair_block for n in range(3 * groups)},
+        blocks={n: per_mode for n in range(2 * groups)},
         out_blocks={0: weight_block},
     )
     arrived, mode_grad = lax.optimization_barrier((arrived, mode_grad))
 
-    (input_grad,) = call(
-        functools.partial(final_kernel, spec_scale),
+    input_grad, local_grad = call(
+        functools.partial(final_kernel, spec_scale, tiles),
         "final",
         (arrived, by_height, back_cols, backward_mix, gate_rows, by_channel),
-        (shape((pixel_rows, width)),),
+        (shape((pixel_rows, width)), shape((channels, channels), F32)),
         [pltpu.VMEM((th, lanes, width), BF16)],
         limit=SMALL,
     )

time: 130 us -> 124 us (0.954)
  blocking collectives: 22 us -> 39.9 us
  starting transfers between devices: 23 us -> 11.1 us
  waiting for transfers between devices: 26.5 us -> 17.7 us
  Pallas kernels: 53.8 us -> 50.5 us
    all_to_all x1 -> x2, blocking collectives: 22 us -> 39.9 us  [exchange(): lax.all_to_all(split, 'tile', split_axis=0, concat_axis=0, tiled=False)]
    ppermute x10 -> x8, waiting for transfers between devices: 26.4 us -> 14.7 us  [swap(): lax.ppermute(values, axis, [(i, i ^ step) for i in range(lax.axis_size(ax...]
    all_to_all x3 -> x2, starting transfers between devices: 13.3 us -> 7.21 us  [exchange(): lax.all_to_all(split, 'tile', split_axis=0, concat_axis=0, tiled=False)]
    ppermute x10 -> x8, starting transfers between devices: 9.76 us -> 3.92 us  [swap(): lax.ppermute(values, axis, [(i, i ^ step) for i in range(lax.axis_size(ax...]
    pallas_call x8, Pallas kernels: 53.8 us -> 50.5 us  [call(): pl.pallas_call(kernel, out_shape=tuple(outs), grid=grid, in_specs=in_spec...]
    all_to_all x3 -> x2, waiting for transfers between devices: 0.06 us -> 3.02 us  [exchange(): lax.all_to_all(split, 'tile', split_axis=0, concat_axis=0, tiled=False)]
    unnamed x31 -> x29, local copies, waits for them, and re-layouts: 2.73 us -> 2.77 us
  transfers between devices with their start and end apart: 13 -> 10, of which waited for: 7 -> 5; matrix products, arithmetic and copies ran while one was open for 1% -> 1% of each run, Pallas kernels for 23% -> 28%
where the time goes in v2:
time: 124 us
  Pallas kernels  50.5 us (41%)
  blocking collectives  39.9 us (32%)
  waiting for transfers between devices  17.7 us (14%)
  starting transfers between devices  11.1 us (9%)
  local copies, waits for them, and re-layouts  2.77 us (2%)
    pallas_call x8, Pallas kernels, call(): pl.pallas_call(kernel, out_shape=tuple(outs), grid=grid, in_specs=in_spec...  50.5 us
    all_to_all x2, blocking collectives, exchange(): lax.all_to_all(split, 'tile', split_axis=0, concat_axis=0, tiled=False)  39.9 us
    ppermute x8, waiting for transfers between devices, swap(): lax.ppermute(values, axis, [(i, i ^ step) for i in range(lax.axis_size(ax...  14.7 us
    all_to_all x2, starting transfers between devices, exchange(): lax.all_to_all(split, 'tile', split_axis=0, concat_axis=0, tiled=False)  7.21 us
    ppermute x8, starting transfers between devices, swap(): lax.ppermute(values, axis, [(i, i ^ step) for i in range(lax.axis_size(ax...  3.92 us
    all_to_all x2, waiting for transfers between devices, exchange(): lax.all_to_all(split, 'tile', split_axis=0, concat_axis=0, tiled=False)  3.02 us
    unnamed x29, local copies, waits for them, and re-layouts  2.77 us
  transfers between devices with their start and end apart: 10, of which 5 were waited for; matrix products, arithmetic and copies ran while one was open for 1% of the time, Pallas kernels for 28%

profile of v2, /device:TPU:0, one launch (start us, length us, event | category | flops | bytes accessed | tf_op | source)
XLA Modules:
  0.0 123.7 jit_solution(11108329757912610528)
XLA Ops:
  0.6 0.0 copy-start.1
  0.6 0.0 copy-start.5
  0.7 0.0 copy-start.7
  0.7 0.0 copy-start.4
  0.7 0.0 copy-start.6
  0.7 3.0 %columns.1 = (bf16[16,128,256]{2,1,0:T(8,128)(2,1)}, bf16[128,2048]{1,0:T(8,128)(2,1)}) custom-call(bf16[256,256]{1,0:T(8,128)(2,1)} %constant.30.order_ref.restore_ref, bf16[128,256]{1,0:T(8,128)(2,1)} %constant.31.table_ref, bf16[2048,256]{1,0:T(8,128)(2,1)} %bitcast.21, bf16[2048,256]{1,0:T(8,128)(2,1)} %bitcast.22, bf16[2048,256]{1,0:T(8,128)(2,1)} %bitcast.23, ...), custom_call_target="tpu_custom_call" | custom-call | tf_op jit(solution)/shard_map/columns/pallas_call | solution.py:410
  3.7 22.0 %all_to_all.20 = bf16[8,16,2048]{2,1,0:T(8,128)(2,1)} all-to-all(bf16[8,16,2048]{2,1,0:T(8,128)(2,1)} %bitcast.32), channel_id=1, replica_groups=mesh['dp'=4,'tile'=8] {'tile'}, dimensions={0} | all-to-all | bytes 1048576 | tf_op jit(solution)/shard_map/all_to_all | solution.py:478
  25.7 9.7 %mix_forward.1 = (bf16[1024,128]{1,0:T(8,128)(2,1)}, bf16[256,1024]{1,0:T(8,128)(2,1)}) custom-call(bf16[128,2048]{1,0:T(8,128)(2,1)} %bitcast.30, bf16[128,128]{1,0:T(8,128)(2,1)} %constant.32.order_ref, bf16[256,128]{1,0:T(8,128)(2,1)} %constant.33.rows_ref, bf16[256,128]{1,0:T(8,128)(2,1)} %constant.34.back_ref, bf16[32768,128]{1,0:T(8,128)(2,1)} %bitcast.18), custom_call_target="tpu_custom_call" | custom-call | tf_op jit(solution)/shard_map/mix_forward/pallas_call | solution.py:410
  35.4 3.6 %all-to-all-start.1 = ((bf16[8,32,1024]{2,1,0:T(8,128)(2,1)}), bf16[8,32,1024]{2,1,0:T(8,128)(2,1)S(1)}, u32[]{:S(2)}, u32[]{:S(2)}) async-start(bf16[8,32,1024]{2,1,0:T(8,128)(2,1)} %bitcast.31), calls=%async_computation.1 | async-start | bytes 1048576 | tf_op jit(solution)/shard_map/all_to_all | solution.py:478
  39.0 1.5 %collective-permute-start.1 = (bf16[1024,128]{1,0:T(8,128)(2,1)}, bf16[1024,128]{1,0:T(8,128)(2,1)S(1)}, u32[]{:S(2)}, u32[]{:S(2)}) collective-permute-start(bf16[1024,128]{1,0:T(8,128)(2,1)} %get-tuple-element.31.refs_0_), channel_id=1, source_target_pairs={{0,16},{8,24},{16,0},{24,8},{1,17},{9,25},{17,1},{25,9},{2,18},{10... | collective-permute-start | bytes 786440 | tf_op jit(solution)/shard_map/ppermute | solution.py:423
  40.5 0.0 collective-permute-start
  40.5 6.1 %collective-permute-done.1.refs_2_ = bf16[1024,128]{1,0:T(8,128)(2,1)S(1)} collective-permute-done((bf16[1024,128]{1,0:T(8,128)(2,1)}, bf16[1024,128]{1,0:T(8,128)(2,1)S(1)}, u32[]{:S(2)}, u32[]{:S(2)}) %collective-permute-start.1) | collective-permute-done | bytes 262176 | tf_op jit(solution)/shard_map/ppermute | solution.py:423
  46.6 0.0 collective-permute-start.2
  46.6 0.8 copy.15
  47.4 2.6 %relayout.1.cot_ref = bf16[16,128,256]{2,1,0:T(8,128)(2,1)} custom-call(bf16[256,256]{1,0:T(8,128)(2,1)} %constant.30.order_ref.restore_ref, bf16[2048,256]{1,0:T(8,128)(2,1)} %bitcast.25, bf16[2048,256]{1,0:T(8,128)(2,1)} %bitcast.26, bf16[2048,256]{1,0:T(8,128)(2,1)} %bitcast.27, bf16[2048,256]{1,0:T(8,128)(2,1)} %bitcast.28), custom_call_target="tpu_custom_call" | custom-call | tf_op jit(solution)/shard_map/relayout/pallas_call | solution.py:410
  50.1 0.1 fusion.4.local_ref
  50.1 3.0 %all-to-all-done.1 = bf16[8,32,1024]{2,1,0:T(8,128)(2,1)S(1)} async-done(((bf16[8,32,1024]{2,1,0:T(8,128)(2,1)}), bf16[8,32,1024]{2,1,0:T(8,128)(2,1)S(1)}, u32[]{:S(2)}, u32[]{:S(2)}) %all-to-all-start.1) | async-done | bytes 524320 | tf_op jit(solution)/shard_map/all_to_all | solution.py:478
  53.2 0.0 copy-done.1
  53.2 0.0 copy-done.5
  53.2 0.0 copy-done.6
  53.2 0.0 copy-start
  53.2 1.2 copy-done
  54.4 6.0 %pixels.1 = (bf16[16,128,256]{2,1,0:T(8,128)(2,1)S(1)}, bf16[128,2048]{1,0:T(8,128)(2,1)S(1)}, f32[64,64]{1,0:T(8,128)S(1)}) custom-call(bf16[256,1024]{1,0:T(8,128)(2,1)S(1)} %bitcast.16, bf16[256,256]{1,0:T(8,128)(2,1)S(1)} %copy-done.1, bf16[128,256]{1,0:T(8,128)(2,1)S(1)} %copy-done.6, bf16[128,128]{1,0:T(8,128)(2,1)S(1)} %fusion.4.local_ref, ...), custom_call_target="tpu_custom_call" | custom-call | tf_op jit(solution)/shard_map/pixels/pallas_call | solution.py:410
  60.4 0.0 collective-permute-done.refs_1_
  60.5 0.0 collective-permute-done.2.refs_3_
  60.5 17.9 %all_to_all.21 = bf16[8,16,2048]{2,1,0:T(8,128)(2,1)S(1)} all-to-all(bf16[8,16,2048]{2,1,0:T(8,128)(2,1)S(1)} %bitcast.17), channel_id=1, replica_groups=mesh['dp'=4,'tile'=8] {'tile'}, dimensions={0} | all-to-all | bytes 1048576 | tf_op jit(solution)/shard_map/all_to_all | solution.py:478
  78.4 0.0 copy-done.7
  78.4 0.6 grad_spectra.1.spec_ref.refs_4_
  79.0 0.1 collective-permute-start.5
  79.1 1.6 %collective-permute-start.6 = (bf16[1024,128]{1,0:T(8,128)(2,1)S(1)}, bf16[1024,128]{1,0:T(8,128)(2,1)S(1)}, u32[]{:S(2)}, u32[]{:S(2)}) collective-permute-start(bf16[1024,128]{1,0:T(8,128)(2,1)S(1)} %grad_spectra.1.spec_ref.refs_4_), channel_id=1, source_target_pairs={{0,16},{8,24},{16,0},{24,8},{1,17},{9,25},{17,1},{25,9},{2,18},{10... | collective-permute-start | bytes 786440 | tf_op jit(solution)/shard_map/ppermute | solution.py:423
  80.7 0.2 collective-permute-start.3
  80.8 1.0 collective-permute-done.3
  81.9 0.5 collective-permute-start.4
  82.4 6.1 %collective-permute-done.4 = f32[64,64]{1,0:T(8,128)S(1)} collective-permute-done((f32[64,64]{1,0:T(8,128)S(1)}, f32[64,64]{1,0:T(8,128)S(1)}, u32[]{:S(2)}, u32[]{:S(2)}) %collective-permute-start.4) | collective-permute-done | bytes 16416 | tf_op jit(solution)/shard_map/ppermute | solution.py:423
  88.5 0.6 add.15.local_ref
  89.1 9.7 %mix_backward.1 = bf16[256,1152]{1,0:T(8,128)(2,1)} custom-call(bf16[1024,128]{1,0:T(8,128)(2,1)} %copy-done.2, bf16[256,128]{1,0:T(8,128)(2,1)} %constant.34.back_ref, f32[64,64]{1,0:T(8,128)} %add.15.local_ref, bf16[32768,128]{1,0:T(8,128)(2,1)} %bitcast.19), custom_call_target="tpu_custom_call" | custom-call | tf_op jit(solution)/shard_map/mix_backward/pallas_call | solution.py:410
  98.9 0.0 collective-permute-done.5.refs_5_
  98.9 0.0 copy-start.10
  98.9 0.0 collective-permute-done.6.refs_6_
  98.9 3.6 %all-to-all-start.3 = ((bf16[8,32,1152]{2,1,0:T(8,128)(2,1)}), bf16[8,32,1152]{2,1,0:T(8,128)(2,1)S(1)}, u32[]{:S(2)}, u32[]{:S(2)}) async-start(bf16[8,32,1152]{2,1,0:T(8,128)(2,1)} %bitcast.29), calls=%async_computation.3 | async-start | bytes 1179648 | tf_op jit(solution)/shard_map/all_to_all | solution.py:478
  102.5 0.0 collective-permute-start.7
  102.6 0.1 fusion.5.local_ref
  102.7 1.4 %collective-permute-done.7.refs_7_ = bf16[1024,128]{1,0:T(8,128)(2,1)S(1)} collective-permute-done((bf16[1024,128]{1,0:T(8,128)(2,1)S(1)}, bf16[1024,128]{1,0:T(8,128)(2,1)S(1)}, u32[]{:S(2)}, u32[]{:S(2)}) %collective-permute-start.7) | collective-permute-done | bytes 262176 | tf_op jit(solution)/shard_map/ppermute | solution.py:423
  104.1 0.0 copy-done.9
  104.1 0.7 copy-done.12
  104.8 16.6 %mode_grad.1 = f32[32768,128]{1,0:T(8,128)} custom-call(bf16[1024,128]{1,0:T(8,128)(2,1)} %get-tuple-element.31.refs_0_, bf16[1024,128]{1,0:T(8,128)(2,1)} %copy-done.9, bf16[1024,128]{1,0:T(8,128)(2,1)} %copy-done.8, bf16[1024,128]{1,0:T(8,128)(2,1)} %collective-permute-done.2.refs_3_, bf16[1024,128]{1,0:T(8,128)(2,1)} %copy-done.2, ...), custom_call_target="tpu_custom_call" | custom-call | tf_op jit(solution)/shard_map/mode_grad/pallas_call | solution.py:410
  121.4 0.0 all-to-all-done.3
  121.4 2.3 %final.1 = (bf16[2048,256]{1,0:T(8,128)(2,1)}, f32[64,64]{1,0:T(8,128)}) custom-call(bf16[256,1152]{1,0:T(8,128)(2,1)S(1)} %bitcast.14, bf16[256,256]{1,0:T(8,128)(2,1)S(1)} %copy-done.1, bf16[128,256]{1,0:T(8,128)(2,1)S(1)} %copy-done.6, bf16[128,128]{1,0:T(8,128)(2,1)S(1)} %fusion.5.local_ref, bf16[16,128,256]{2,1,0:T(8,128)(2,1)S(1)} %get-tuple-element.39.grad_ref, ...), custom_call_target="tpu_custom_call" | custom-call | tf_op jit(solution)/shard_map/final/pallas_call | solution.py:410
  (15 shorter events, 0.0 us)
Async XLA Ops:
  0.6 52.5 %copy-start.1 = (bf16[256,256]{1,0:T(8,128)(2,1)S(1)}, bf16[256,256]{1,0:T(8,128)(2,1)}, u32[]{:S(2)}) copy-start(bf16[256,256]{1,0:T(8,128)(2,1)} %constant.30.order_ref.restore_ref) | copy-start | bytes 393220
  0.6 52.5 %copy-start.5 = (bf16[128,256]{1,0:T(8,128)(2,1)S(1)}, bf16[128,256]{1,0:T(8,128)(2,1)}, u32[]{:S(2)}) copy-start(bf16[128,256]{1,0:T(8,128)(2,1)} %constant.31.table_ref) | copy-start | bytes 196612
  0.7 77.7 %copy-start.7 = (bf16[128,128]{1,0:T(8,128)(2,1)S(1)}, bf16[128,128]{1,0:T(8,128)(2,1)}, u32[]{:S(2)}) copy-start(bf16[128,128]{1,0:T(8,128)(2,1)} %constant.32.order_ref) | copy-start | bytes 98308
  0.7 77.7 %copy-start.4 = (bf16[256,128]{1,0:T(8,128)(2,1)S(1)}, bf16[256,128]{1,0:T(8,128)(2,1)}, u32[]{:S(2)}) copy-start(bf16[256,128]{1,0:T(8,128)(2,1)} %constant.33.rows_ref) | copy-start | bytes 196612
  0.7 52.5 %copy-start.6 = (bf16[128,256]{1,0:T(8,128)(2,1)S(1)}, bf16[128,256]{1,0:T(8,128)(2,1)}, u32[]{:S(2)}) copy-start(bf16[128,256]{1,0:T(8,128)(2,1)} %constant.35.back_ref) | copy-start | bytes 196612
  3.6 49.5 %copy-start.3 = (bf16[16,128,256]{2,1,0:T(8,128)(2,1)S(1)}, bf16[16,128,256]{2,1,0:T(8,128)(2,1)}, u32[]{:S(2)}) copy-start(bf16[16,128,256]{2,1,0:T(8,128)(2,1)} %get-tuple-element.25.field_ref) | copy-start | bytes 3145732
  3.7 98.9 %copy-start.13 = (bf16[64,64]{1,0:T(8,128)(2,1)S(1)}, bf16[64,64]{1,0:T(8,128)(2,1)}, u32[]{:S(2)}) copy-start(bf16[64,64]{1,0:T(8,128)(2,1)} %param.15) | copy-start | bytes 24580
  35.4 17.8 %all-to-all-start.1 = ((bf16[8,32,1024]{2,1,0:T(8,128)(2,1)}), bf16[8,32,1024]{2,1,0:T(8,128)(2,1)S(1)}, u32[]{:S(2)}, u32[]{:S(2)}) async-start(bf16[8,32,1024]{2,1,0:T(8,128)(2,1)} %bitcast.31), calls=%async_computation.1 | async-start | bytes 1048576 | tf_op jit(solution)/shard_map/all_to_all | solution.py:478
  39.0 7.6 %collective-permute-start.1 = (bf16[1024,128]{1,0:T(8,128)(2,1)}, bf16[1024,128]{1,0:T(8,128)(2,1)S(1)}, u32[]{:S(2)}, u32[]{:S(2)}) collective-permute-start(bf16[1024,128]{1,0:T(8,128)(2,1)} %get-tuple-element.31.refs_0_), channel_id=1, source_target_pairs={{0,16},{8,24},{16,0},{24,8},{1,17},{9,25},{17,1},{25,9},{2,18},{10... | collective-permute-start | bytes 786440 | tf_op jit(solution)/shard_map/ppermute | solution.py:423
  40.5 19.9 %collective-permute-start = (bf16[1024,128]{1,0:T(8,128)(2,1)}, bf16[1024,128]{1,0:T(8,128)(2,1)S(1)}, u32[]{:S(2)}, u32[]{:S(2)}) collective-permute-start(bf16[1024,128]{1,0:T(8,128)(2,1)} %get-tuple-element.31.refs_0_), channel_id=1, source_target_pairs={{0,8},{8,0},{16,24},{24,16},{1,9},{9,1},{17,25},{25,17},{2,10},{10... | collective-permute-start | bytes 786440 | tf_op jit(solution)/shard_map/ppermute | solution.py:423
  46.6 57.5 %copy-start.8 = (bf16[1024,128]{1,0:T(8,128)(2,1)}, bf16[1024,128]{1,0:T(8,128)(2,1)S(1)}, u32[]{:S(2)}) copy-start(bf16[1024,128]{1,0:T(8,128)(2,1)S(1)} %collective-permute-done.1.refs_2_) | copy-start | bytes 786436
  46.6 13.8 %collective-permute-start.2 = (bf16[1024,128]{1,0:T(8,128)(2,1)S(1)}, bf16[1024,128]{1,0:T(8,128)(2,1)}, u32[]{:S(2)}, u32[]{:S(2)}) collective-permute-start(bf16[1024,128]{1,0:T(8,128)(2,1)S(1)} %collective-permute-done.1.refs_2_), channel_id=1, source_target_pairs={{0,8},{8,0},{16,24},{24,16},{1,9},{9,1},{17,25},{25,17},{2,10},{10... | collective-permute-start | bytes 786440 | tf_op jit(solution)/shard_map/ppermute | solution.py:423
  53.2 1.2 copy-start
  60.4 43.6 %copy-start.9 = (bf16[1024,128]{1,0:T(8,128)(2,1)}, bf16[1024,128]{1,0:T(8,128)(2,1)S(1)}, u32[]{:S(2)}) copy-start(bf16[1024,128]{1,0:T(8,128)(2,1)S(1)} %collective-permute-done.refs_1_) | copy-start | bytes 786436
  79.0 10.1 %copy-start.2 = (bf16[1024,128]{1,0:T(8,128)(2,1)}, bf16[1024,128]{1,0:T(8,128)(2,1)S(1)}, u32[]{:S(2)}) copy-start(bf16[1024,128]{1,0:T(8,128)(2,1)S(1)} %grad_spectra.1.spec_ref.refs_4_) | copy-start | bytes 786436
  79.0 19.9 %collective-permute-start.5 = (bf16[1024,128]{1,0:T(8,128)(2,1)S(1)}, bf16[1024,128]{1,0:T(8,128)(2,1)S(1)}, u32[]{:S(2)}, u32[]{:S(2)}) collective-permute-start(bf16[1024,128]{1,0:T(8,128)(2,1)S(1)} %grad_spectra.1.spec_ref.refs_4_), channel_id=1, source_target_pairs={{0,8},{8,0},{16,24},{24,16},{1,9},{9,1},{17,25},{25,17},{2,10},{10... | collective-permute-start | bytes 786440 | tf_op jit(solution)/shard_map/ppermute | solution.py:423
  79.1 19.8 %collective-permute-start.6 = (bf16[1024,128]{1,0:T(8,128)(2,1)S(1)}, bf16[1024,128]{1,0:T(8,128)(2,1)S(1)}, u32[]{:S(2)}, u32[]{:S(2)}) collective-permute-start(bf16[1024,128]{1,0:T(8,128)(2,1)S(1)} %grad_spectra.1.spec_ref.refs_4_), channel_id=1, source_target_pairs={{0,16},{8,24},{16,0},{24,8},{1,17},{9,25},{17,1},{25,9},{2,18},{10... | collective-permute-start | bytes 786440 | tf_op jit(solution)/shard_map/ppermute | solution.py:423
  80.7 1.2 collective-permute-start.3
  81.9 6.6 %collective-permute-start.4 = (f32[64,64]{1,0:T(8,128)S(1)}, f32[64,64]{1,0:T(8,128)S(1)}, u32[]{:S(2)}, u32[]{:S(2)}) collective-permute-start(f32[64,64]{1,0:T(8,128)S(1)} %add.14), channel_id=1, source_target_pairs={{0,16},{8,24},{16,0},{24,8},{1,17},{9,25},{17,1},{25,9},{2,18},{10... | collective-permute-start | bytes 49160 | tf_op jit(solution)/shard_map/ppermute | solution.py:423
  98.9 5.2 %copy-start.10 = (bf16[1024,128]{1,0:T(8,128)(2,1)}, bf16[1024,128]{1,0:T(8,128)(2,1)S(1)}, u32[]{:S(2)}) copy-start(bf16[1024,128]{1,0:T(8,128)(2,1)S(1)} %collective-permute-done.5.refs_5_) | copy-start | bytes 786436
  98.9 5.2 %copy-start.11 = (bf16[1024,128]{1,0:T(8,128)(2,1)}, bf16[1024,128]{1,0:T(8,128)(2,1)S(1)}, u32[]{:S(2)}) copy-start(bf16[1024,128]{1,0:T(8,128)(2,1)S(1)} %collective-permute-done.6.refs_6_) | copy-start | bytes 786436
  98.9 22.5 %all-to-all-start.3 = ((bf16[8,32,1152]{2,1,0:T(8,128)(2,1)}), bf16[8,32,1152]{2,1,0:T(8,128)(2,1)S(1)}, u32[]{:S(2)}, u32[]{:S(2)}) async-start(bf16[8,32,1152]{2,1,0:T(8,128)(2,1)} %bitcast.29), calls=%async_computation.3 | async-start | bytes 1179648 | tf_op jit(solution)/shard_map/all_to_all | solution.py:478
  102.5 1.6 %collective-permute-start.7 = (bf16[1024,128]{1,0:T(8,128)(2,1)S(1)}, bf16[1024,128]{1,0:T(8,128)(2,1)S(1)}, u32[]{:S(2)}, u32[]{:S(2)}) collective-permute-start(bf16[1024,128]{1,0:T(8,128)(2,1)S(1)} %collective-permute-done.6.refs_6_), channel_id=1, source_target_pairs={{0,8},{8,0},{16,24},{24,16},{1,9},{9,1},{17,25},{25,17},{2,10},{10... | collective-permute-start | bytes 786440 | tf_op jit(solution)/shard_map/ppermute | solution.py:423
  104.1 0.7 copy-start.12

commit v3 on v2

--- a/solution.py
+++ b/solution.py
@@ -77,9 +77,11 @@
 
 
 def gelu_slope(values):
-    size = jnp.abs(values)
-    expo = jnp.exp(-0.5 * values * values)
-    t = 1.0 / (1.0 + (0.3275911 / math.sqrt(2.0)) * size)
+    root = values * math.sqrt(0.5 * math.log2(math.e))
+    expo = jnp.exp2(-(root * root))
+    base = 1.0 + (0.3275911 / math.sqrt(2.0)) * jnp.abs(values)
+    t = pl.reciprocal(base, approx=True)
+    t = t * (2.0 - base * t)
     poly = 0.5 * 1.061405429
     for factor in (-1.453152027, 1.421413741, -0.284496736, 0.254829592):
         poly = poly * t + 0.5 * factor
@@ -186,6 +188,19 @@
             send_ref[:, q * lanes : (q + 1) * lanes] = dot(back_ref[...], mixed, ((1,), (1,))).astype(BF16)
 
 
+def fetch(sources, targets, sems):
+    moves = [
+        pltpu.make_async_copy(source, target, sems.at[n]) for n, (source, target) in enumerate(zip(sources, targets))
+    ]
+
+    @pl.when(pl.program_id(0) == 0)
+    def _():
+        for move in moves:
+            move.start()
+
+    return moves
+
+
 def fetch_weights(source_ref, weights, sems):
     q = pl.program_id(0)
     owned = sems.shape[0]
@@ -207,17 +222,22 @@
     return move(q), weights.at[pl.ds(pl.multiple_of(q * size, size), size), :]
 
 
-def forward_kernel(scale, samples, owned, recv_ref, order_ref, rows_ref, back_ref, source_ref, *rest):
-    spec_ref, send_ref, real, imag, sums, weights, sems = rest
+def forward_kernel(scale, samples, owned, *rest):
+    sources, source_ref, spec_ref, send_ref, real, imag, sums, weights, sems = rest[:4], *rest[4:12]
+    targets, early = rest[12:16], rest[16]
+    recv_ref, order_ref, rows_ref, back_ref = targets
     _, _, outs, both = sums.shape
     channels = weights.shape[0] // outs // owned
     half = both // 2
     lanes = samples * channels
     q = pl.program_id(0)
+    moves = fetch(sources, targets, early)
     coming, weight_ref = fetch_weights(source_ref, weights, sems)
 
     @pl.when(q == 0)
     def _():
+        for move in moves:
+            move.wait()
         spectra_into(scale, owned, lanes, recv_ref, order_ref, rows_ref, spec_ref)
         real[...], imag[...] = duplicates(spec_ref[...], half)
         sums[...] = jnp.zeros_like(sums)
@@ -256,17 +276,22 @@
     finish(back_ref, sums, send_ref, mix)
 
 
-def backward_kernel(samples, tiles, spec_ref, back_ref, local_ref, source_ref, *rest):
-    send_ref, real, imag, sums, weights, sems = rest
+def backward_kernel(samples, tiles, *rest):
+    sources, source_ref, send_ref, real, imag, sums, weights, sems = rest[:3], *rest[3:10]
+    targets, early = rest[10:13], rest[13]
+    spec_ref, back_ref, local_ref = targets
     channels, both = sums.shape[2] // ROWS, sums.shape[3]
     outs = weights.shape[0] // channels // sums.shape[0]
     half = both // 2
     lanes = samples * outs
     q = pl.program_id(0)
+    moves = fetch(sources, targets, early)
     coming, weight_ref = fetch_weights(source_ref, weights, sems)
 
     @pl.when(q == 0)
     def _():
+        for move in moves:
+            move.wait()
         first, second = duplicates(spec_ref[...], half)
         real[...], imag[...] = first.astype(BF16), second.astype(BF16)
         extent = send_ref.shape[0] // tiles
@@ -510,6 +535,10 @@
         (field_shape,),
         blocks=field_blocks(1),
     )
+    def early(*operands):
+        kept = [pltpu.VMEM(operand.shape, operand.dtype) for operand in operands]
+        return kept + [pltpu.SemaphoreType.DMA((len(operands),))]
+
     spectra, send = call(
         functools.partial(forward_kernel, spec_scale, samples, owned),
         "mix_forward",
@@ -520,9 +549,10 @@
             pltpu.VMEM((owned * lanes, both), F32),
             pltpu.VMEM((owned, 2 * samples, channels, both), F32),
             *weight_scratch,
+            *early(arrived, by_mode, rows, back_rows),
         ],
         grid=(owned,),
-        blocks={4: in_place},
+        blocks={n: in_place for n in range(5)},
     )
     all_spectra = gather_far(gather_near(spectra, "dp"), "dp")
     arrived = exchange(send)
@@ -540,8 +570,7 @@
         limit=SMALL,
     )
     send, *all_spectra = lax.optimization_barrier((send, *all_spectra))
-    arrived = exchange(send)
-    local_sum = sum_over(local_sum, "dp")
+    arrived, local_sum = lax.optimization_barrier((exchange(send), sum_over(local_sum, "dp")))
     (grad_spectra,) = call(
         functools.partial(spectra_kernel, mode_scale, owned, lanes),
         "grad_spectra",
@@ -560,9 +589,10 @@
             pltpu.VMEM((owned * lanes, both), BF16),
             pltpu.VMEM((owned, 2 * samples, channels * ROWS, both), F32),
             *weight_scratch,
+            *early(grad_spectra, back_rows, local_sum),
         ],
         grid=(owned,),
-        blocks={3: in_place},
+        blocks={n: in_place for n in range(4)},
     )
     send, near = lax.optimization_barrier((send, near))
     all_grads = gather_far(near, "dp")

time: 124 us -> 117 us (0.944)
  blocking collectives: 39.9 us -> 22 us
  waiting for transfers between devices: 17.7 us -> 22.7 us
  starting transfers between devices: 11.1 us -> 15.8 us
    all_to_all x2 -> x1, blocking collectives: 39.9 us -> 22 us  [exchange(): lax.all_to_all(split, 'tile', split_axis=0, concat_axis=0, tiled=False)]
    all_to_all x2 -> x3, waiting for transfers between devices: 3.02 us -> 11.7 us  [exchange(): lax.all_to_all(split, 'tile', split_axis=0, concat_axis=0, tiled=False)]
    all_to_all x2 -> x3, starting transfers between devices: 7.21 us -> 10.9 us  [exchange(): lax.all_to_all(split, 'tile', split_axis=0, concat_axis=0, tiled=False)]
    ppermute x8, waiting for transfers between devices: 14.7 us -> 11 us  [swap(): lax.ppermute(values, axis, [(i, i ^ step) for i in range(lax.axis_size(ax...]
    unnamed x29 -> x27, local copies, waits for them, and re-layouts: 2.77 us -> 2.78 us
  transfers between devices with their start and end apart: 10 -> 11, of which waited for: 5 -> 6; matrix products, arithmetic and copies ran while one was open for 1% -> 1% of each run, Pallas kernels for 28% -> 31%
where the time goes in v3:
time: 117 us
  Pallas kernels  51.6 us (44%)
  waiting for transfers between devices  22.7 us (19%)
  blocking collectives  22 us (19%)
  starting transfers between devices  15.8 us (14%)
  local copies, waits for them, and re-layouts  2.78 us (2%)
    pallas_call x8, Pallas kernels, call(): pl.pallas_call(kernel, out_shape=tuple(outs), grid=grid, in_specs=in_spec...  51.6 us
    all_to_all x1, blocking collectives, exchange(): lax.all_to_all(split, 'tile', split_axis=0, concat_axis=0, tiled=False)  22 us
    all_to_all x3, waiting for transfers between devices, exchange(): lax.all_to_all(split, 'tile', split_axis=0, concat_axis=0, tiled=False)  11.7 us
    ppermute x8, waiting for transfers between devices, swap(): lax.ppermute(values, axis, [(i, i ^ step) for i in range(lax.axis_size(ax...  11 us
    all_to_all x3, starting transfers between devices, exchange(): lax.all_to_all(split, 'tile', split_axis=0, concat_axis=0, tiled=False)  10.9 us
    ppermute x8, starting transfers between devices, swap(): lax.ppermute(values, axis, [(i, i ^ step) for i in range(lax.axis_size(ax...  4.87 us
    unnamed x27, local copies, waits for them, and re-layouts  2.78 us
  transfers between devices with their start and end apart: 11, of which 6 were waited for; matrix products, arithmetic and copies ran while one was open for 1% of the time, Pallas kernels for 31%

profile of v3, /device:TPU:0, one launch (start us, length us, event | category | flops | bytes accessed | tf_op | source)
XLA Modules:
  0.0 116.5 jit_solution(1666252580942241563)
XLA Ops:
  0.6 0.0 copy-start.1
  0.6 0.0 copy-start.5
  0.7 0.0 copy-start.7
  0.7 0.0 copy-start.4
  0.7 0.0 copy-start.6
  0.7 3.0 %columns.1 = (bf16[16,128,256]{2,1,0:T(8,128)(2,1)}, bf16[128,2048]{1,0:T(8,128)(2,1)}) custom-call(bf16[256,256]{1,0:T(8,128)(2,1)} %constant.30.order_ref.restore_ref, bf16[128,256]{1,0:T(8,128)(2,1)} %constant.31.table_ref, bf16[2048,256]{1,0:T(8,128)(2,1)} %bitcast.20, bf16[2048,256]{1,0:T(8,128)(2,1)} %bitcast.21, bf16[2048,256]{1,0:T(8,128)(2,1)} %bitcast.22, ...), custom_call_target="tpu_custom_call" | custom-call | tf_op jit(solution)/shard_map/columns/pallas_call | solution.py:435
  3.7 22.0 %all_to_all.20 = bf16[8,16,2048]{2,1,0:T(8,128)(2,1)} all-to-all(bf16[8,16,2048]{2,1,0:T(8,128)(2,1)} %bitcast.31), channel_id=1, replica_groups=mesh['dp'=4,'tile'=8] {'tile'}, dimensions={0} | all-to-all | bytes 1048576 | tf_op jit(solution)/shard_map/all_to_all | solution.py:503
  25.7 10.2 %mix_forward.1 = (bf16[1024,128]{1,0:T(8,128)(2,1)}, bf16[256,1024]{1,0:T(8,128)(2,1)}) custom-call(bf16[128,2048]{1,0:T(8,128)(2,1)} %bitcast.29, bf16[128,128]{1,0:T(8,128)(2,1)} %constant.32.rest_1_.order_ref, bf16[256,128]{1,0:T(8,128)(2,1)} %constant.33.rest_2_.rows_ref, bf16[256,128]{1,0:T(8,128)(2,1)} %constant.34.rest_3_.rest_1_, ...), custom_call_target="tpu_custom_call" | custom-call | tf_op jit(solution)/shard_map/mix_forward/pallas_call | solution.py:435
  35.8 3.6 %all-to-all-start.1 = ((bf16[8,32,1024]{2,1,0:T(8,128)(2,1)}), bf16[8,32,1024]{2,1,0:T(8,128)(2,1)S(1)}, u32[]{:S(2)}, u32[]{:S(2)}) async-start(bf16[8,32,1024]{2,1,0:T(8,128)(2,1)} %bitcast.30), calls=%async_computation.1 | async-start | bytes 1048576 | tf_op jit(solution)/shard_map/all_to_all | solution.py:503
  39.4 1.5 %collective-permute-start.1 = (bf16[1024,128]{1,0:T(8,128)(2,1)}, bf16[1024,128]{1,0:T(8,128)(2,1)S(1)}, u32[]{:S(2)}, u32[]{:S(2)}) collective-permute-start(bf16[1024,128]{1,0:T(8,128)(2,1)} %get-tuple-element.35.refs_0_), channel_id=1, source_target_pairs={{0,16},{8,24},{16,0},{24,8},{1,17},{9,25},{17,1},{25,9},{2,18},{10... | collective-permute-start | bytes 786440 | tf_op jit(solution)/shard_map/ppermute | solution.py:448
  41.0 0.0 collective-permute-start
  41.0 6.1 %collective-permute-done.1.refs_2_ = bf16[1024,128]{1,0:T(8,128)(2,1)S(1)} collective-permute-done((bf16[1024,128]{1,0:T(8,128)(2,1)}, bf16[1024,128]{1,0:T(8,128)(2,1)S(1)}, u32[]{:S(2)}, u32[]{:S(2)}) %collective-permute-start.1) | collective-permute-done | bytes 262176 | tf_op jit(solution)/shard_map/ppermute | solution.py:448
  47.1 0.0 collective-permute-start.2
  47.1 0.8 copy.15
  47.9 2.6 %relayout.1.cot_ref = bf16[16,128,256]{2,1,0:T(8,128)(2,1)} custom-call(bf16[256,256]{1,0:T(8,128)(2,1)} %constant.30.order_ref.restore_ref, bf16[2048,256]{1,0:T(8,128)(2,1)} %bitcast.24, bf16[2048,256]{1,0:T(8,128)(2,1)} %bitcast.25, bf16[2048,256]{1,0:T(8,128)(2,1)} %bitcast.26, bf16[2048,256]{1,0:T(8,128)(2,1)} %bitcast.27), custom_call_target="tpu_custom_call" | custom-call | tf_op jit(solution)/shard_map/relayout/pallas_call | solution.py:435
  50.5 0.1 fusion.4.local_ref
  50.6 3.0 %all-to-all-done.1 = bf16[8,32,1024]{2,1,0:T(8,128)(2,1)S(1)} async-done(((bf16[8,32,1024]{2,1,0:T(8,128)(2,1)}), bf16[8,32,1024]{2,1,0:T(8,128)(2,1)S(1)}, u32[]{:S(2)}, u32[]{:S(2)}) %all-to-all-start.1) | async-done | bytes 524320 | tf_op jit(solution)/shard_map/all_to_all | solution.py:503
  53.6 0.0 copy-done.1
  53.6 0.0 copy-start
  53.7 1.2 %copy-done = bf16[16,128,256]{2,1,0:T(8,128)(2,1)S(1)} copy-done((bf16[16,128,256]{2,1,0:T(8,128)(2,1)S(1)}, bf16[16,128,256]{2,1,0:T(8,128)(2,1)}, u32[]{:S(2)}) %copy-start) | copy-done | bytes 1048600
  54.9 6.9 %pixels.1 = (bf16[16,128,256]{2,1,0:T(8,128)(2,1)S(1)}, bf16[128,2048]{1,0:T(8,128)(2,1)}, f32[64,64]{1,0:T(8,128)S(1)}) custom-call(bf16[256,1024]{1,0:T(8,128)(2,1)S(1)} %bitcast.16, bf16[256,256]{1,0:T(8,128)(2,1)S(1)} %copy-done.1, bf16[128,256]{1,0:T(8,128)(2,1)S(1)} %copy-done.6, bf16[128,128]{1,0:T(8,128)(2,1)S(1)} %fusion.4.local_ref, ...), custom_call_target="tpu_custom_call" | custom-call | tf_op jit(solution)/shard_map/pixels/pallas_call | solution.py:435
  61.8 0.0 collective-permute-done.refs_1_
  61.8 0.0 collective-permute-done.2.refs_3_
  61.8 3.6 %all-to-all-start.2 = ((bf16[8,16,2048]{2,1,0:T(8,128)(2,1)}), bf16[8,16,2048]{2,1,0:T(8,128)(2,1)S(1)}, u32[]{:S(2)}, u32[]{:S(2)}) async-start(bf16[8,16,2048]{2,1,0:T(8,128)(2,1)} %bitcast.8), calls=%async_computation.2 | async-start | bytes 1048576 | tf_op jit(solution)/shard_map/all_to_all | solution.py:503
  65.4 0.0 collective-permute-start.3
  65.5 1.2 %collective-permute-done.3 = f32[64,64]{1,0:T(8,128)S(1)} collective-permute-done((f32[64,64]{1,0:T(8,128)S(1)}, f32[64,64]{1,0:T(8,128)S(1)}, u32[]{:S(2)}, u32[]{:S(2)}) %collective-permute-start.3) | collective-permute-done | bytes 16416 | tf_op jit(solution)/shard_map/ppermute | solution.py:448
  66.7 1.5 %collective-permute-start.4 = (f32[64,64]{1,0:T(8,128)S(1)}, f32[64,64]{1,0:T(8,128)S(1)}, u32[]{:S(2)}, u32[]{:S(2)}) collective-permute-start(f32[64,64]{1,0:T(8,128)S(1)} %add.14), channel_id=1, source_target_pairs={{0,16},{8,24},{16,0},{24,8},{1,17},{9,25},{17,1},{25,9},{2,18},{10... | collective-permute-start | bytes 49160 | tf_op jit(solution)/shard_map/ppermute | solution.py:448
  68.2 2.4 %collective-permute-done.4 = f32[64,64]{1,0:T(8,128)S(1)} collective-permute-done((f32[64,64]{1,0:T(8,128)S(1)}, f32[64,64]{1,0:T(8,128)S(1)}, u32[]{:S(2)}, u32[]{:S(2)}) %collective-permute-start.4) | collective-permute-done | bytes 16416 | tf_op jit(solution)/shard_map/ppermute | solution.py:448
  70.6 0.6 add.15.rest_2_
  71.2 8.7 %all-to-all-done.2 = bf16[8,16,2048]{2,1,0:T(8,128)(2,1)S(1)} async-done(((bf16[8,16,2048]{2,1,0:T(8,128)(2,1)}), bf16[8,16,2048]{2,1,0:T(8,128)(2,1)S(1)}, u32[]{:S(2)}, u32[]{:S(2)}) %all-to-all-start.2) | async-done | bytes 524320 | tf_op jit(solution)/shard_map/all_to_all | solution.py:503
  79.9 0.0 copy-done.4
  79.9 0.6 grad_spectra.1.rest_0_.refs_4_
  80.5 0.1 collective-permute-start.5
  80.6 1.6 %collective-permute-start.6 = (bf16[1024,128]{1,0:T(8,128)(2,1)S(1)}, bf16[1024,128]{1,0:T(8,128)(2,1)S(1)}, u32[]{:S(2)}, u32[]{:S(2)}) collective-permute-start(bf16[1024,128]{1,0:T(8,128)(2,1)S(1)} %grad_spectra.1.rest_0_.refs_4_), channel_id=1, source_target_pairs={{0,16},{8,24},{16,0},{24,8},{1,17},{9,25},{17,1},{25,9},{2,18},{10... | collective-permute-start | bytes 786440 | tf_op jit(solution)/shard_map/ppermute | solution.py:448
  82.2 9.5 %mix_backward.1 = bf16[256,1152]{1,0:T(8,128)(2,1)} custom-call(bf16[1024,128]{1,0:T(8,128)(2,1)} %copy-done.2, bf16[256,128]{1,0:T(8,128)(2,1)} %constant.34.rest_3_.rest_1_, f32[64,64]{1,0:T(8,128)} %add.15.rest_2_, bf16[32768,128]{1,0:T(8,128)(2,1)} %bitcast.18), custom_call_target="tpu_custom_call" | custom-call | tf_op jit(solution)/shard_map/mix_backward/pallas_call | solution.py:435
  91.6 0.0 collective-permute-done.5.refs_5_
  91.7 0.0 copy-start.9
  91.7 0.0 collective-permute-done.6.refs_6_
  91.7 3.6 %all-to-all-start.3 = ((bf16[8,32,1152]{2,1,0:T(8,128)(2,1)}), bf16[8,32,1152]{2,1,0:T(8,128)(2,1)S(1)}, u32[]{:S(2)}, u32[]{:S(2)}) async-start(bf16[8,32,1152]{2,1,0:T(8,128)(2,1)} %bitcast.28), calls=%async_computation.3 | async-start | bytes 1179648 | tf_op jit(solution)/shard_map/all_to_all | solution.py:503
  95.3 0.1 collective-permute-start.7
  95.5 0.1 fusion.5.local_ref
  95.6 1.3 %collective-permute-done.7.refs_7_ = bf16[1024,128]{1,0:T(8,128)(2,1)S(1)} collective-permute-done((bf16[1024,128]{1,0:T(8,128)(2,1)S(1)}, bf16[1024,128]{1,0:T(8,128)(2,1)S(1)}, u32[]{:S(2)}, u32[]{:S(2)}) %collective-permute-start.7) | collective-permute-done | bytes 262176 | tf_op jit(solution)/shard_map/ppermute | solution.py:448
  96.9 0.0 copy-done.8
  96.9 0.0 copy-done.10
  96.9 0.7 copy-done.11
  97.6 16.6 %mode_grad.1 = f32[32768,128]{1,0:T(8,128)} custom-call(bf16[1024,128]{1,0:T(8,128)(2,1)} %get-tuple-element.35.refs_0_, bf16[1024,128]{1,0:T(8,128)(2,1)} %collective-permute-done.refs_1_, bf16[1024,128]{1,0:T(8,128)(2,1)} %copy-done.8, bf16[1024,128]{1,0:T(8,128)(2,1)} %collective-permute-done.2.refs_3_, bf16[1024,128]{1,0:T(8,128)(2,1)} %copy-done.2, ...), custom_call_target="tpu_custom_call" | custom-call | tf_op jit(solution)/shard_map/mode_grad/pallas_call | solution.py:435
  114.2 0.0 all-to-all-done.3
  114.2 2.3 %final.1 = (bf16[2048,256]{1,0:T(8,128)(2,1)}, f32[64,64]{1,0:T(8,128)}) custom-call(bf16[256,1152]{1,0:T(8,128)(2,1)S(1)} %bitcast.14, bf16[256,256]{1,0:T(8,128)(2,1)S(1)} %copy-done.1, bf16[128,256]{1,0:T(8,128)(2,1)S(1)} %copy-done.6, bf16[128,128]{1,0:T(8,128)(2,1)S(1)} %fusion.5.local_ref, bf16[16,128,256]{2,1,0:T(8,128)(2,1)S(1)} %get-tuple-element.43.grad_ref, ...), custom_call_target="tpu_custom_call" | custom-call | tf_op jit(solution)/shard_map/final/pallas_call | solution.py:435
  (14 shorter events, 0.0 us)
Async XLA Ops:
  0.6 53.0 %copy-start.1 = (bf16[256,256]{1,0:T(8,128)(2,1)S(1)}, bf16[256,256]{1,0:T(8,128)(2,1)}, u32[]{:S(2)}) copy-start(bf16[256,256]{1,0:T(8,128)(2,1)} %constant.30.order_ref.restore_ref) | copy-start | bytes 393220
  0.6 53.0 %copy-start.5 = (bf16[128,256]{1,0:T(8,128)(2,1)S(1)}, bf16[128,256]{1,0:T(8,128)(2,1)}, u32[]{:S(2)}) copy-start(bf16[128,256]{1,0:T(8,128)(2,1)} %constant.31.table_ref) | copy-start | bytes 196612
  0.7 79.2 %copy-start.7 = (bf16[128,128]{1,0:T(8,128)(2,1)S(1)}, bf16[128,128]{1,0:T(8,128)(2,1)}, u32[]{:S(2)}) copy-start(bf16[128,128]{1,0:T(8,128)(2,1)} %constant.32.rest_1_.order_ref) | copy-start | bytes 98308
  0.7 79.2 %copy-start.4 = (bf16[256,128]{1,0:T(8,128)(2,1)S(1)}, bf16[256,128]{1,0:T(8,128)(2,1)}, u32[]{:S(2)}) copy-start(bf16[256,128]{1,0:T(8,128)(2,1)} %constant.33.rest_2_.rows_ref) | copy-start | bytes 196612
  0.7 53.0 %copy-start.6 = (bf16[128,256]{1,0:T(8,128)(2,1)S(1)}, bf16[128,256]{1,0:T(8,128)(2,1)}, u32[]{:S(2)}) copy-start(bf16[128,256]{1,0:T(8,128)(2,1)} %constant.35.back_ref) | copy-start | bytes 196612
  3.6 50.0 %copy-start.3 = (bf16[16,128,256]{2,1,0:T(8,128)(2,1)S(1)}, bf16[16,128,256]{2,1,0:T(8,128)(2,1)}, u32[]{:S(2)}) copy-start(bf16[16,128,256]{2,1,0:T(8,128)(2,1)} %get-tuple-element.27.field_ref) | copy-start | bytes 3145732
  3.7 91.8 %copy-start.12 = (bf16[64,64]{1,0:T(8,128)(2,1)S(1)}, bf16[64,64]{1,0:T(8,128)(2,1)}, u32[]{:S(2)}) copy-start(bf16[64,64]{1,0:T(8,128)(2,1)} %param.15) | copy-start | bytes 24580
  35.8 17.8 %all-to-all-start.1 = ((bf16[8,32,1024]{2,1,0:T(8,128)(2,1)}), bf16[8,32,1024]{2,1,0:T(8,128)(2,1)S(1)}, u32[]{:S(2)}, u32[]{:S(2)}) async-start(bf16[8,32,1024]{2,1,0:T(8,128)(2,1)} %bitcast.30), calls=%async_computation.1 | async-start | bytes 1048576 | tf_op jit(solution)/shard_map/all_to_all | solution.py:503
  39.4 7.6 %collective-permute-start.1 = (bf16[1024,128]{1,0:T(8,128)(2,1)}, bf16[1024,128]{1,0:T(8,128)(2,1)S(1)}, u32[]{:S(2)}, u32[]{:S(2)}) collective-permute-start(bf16[1024,128]{1,0:T(8,128)(2,1)} %get-tuple-element.35.refs_0_), channel_id=1, source_target_pairs={{0,16},{8,24},{16,0},{24,8},{1,17},{9,25},{17,1},{25,9},{2,18},{10... | collective-permute-start | bytes 786440 | tf_op jit(solution)/shard_map/ppermute | solution.py:448
  41.0 20.8 %collective-permute-start = (bf16[1024,128]{1,0:T(8,128)(2,1)}, bf16[1024,128]{1,0:T(8,128)(2,1)}, u32[]{:S(2)}, u32[]{:S(2)}) collective-permute-start(bf16[1024,128]{1,0:T(8,128)(2,1)} %get-tuple-element.35.refs_0_), channel_id=1, source_target_pairs={{0,8},{8,0},{16,24},{24,16},{1,9},{9,1},{17,25},{25,17},{2,10},{10... | collective-permute-start | bytes 786440 | tf_op jit(solution)/shard_map/ppermute | solution.py:448
  47.1 49.8 %copy-start.8 = (bf16[1024,128]{1,0:T(8,128)(2,1)}, bf16[1024,128]{1,0:T(8,128)(2,1)S(1)}, u32[]{:S(2)}) copy-start(bf16[1024,128]{1,0:T(8,128)(2,1)S(1)} %collective-permute-done.1.refs_2_) | copy-start | bytes 786436
  47.1 14.7 %collective-permute-start.2 = (bf16[1024,128]{1,0:T(8,128)(2,1)S(1)}, bf16[1024,128]{1,0:T(8,128)(2,1)}, u32[]{:S(2)}, u32[]{:S(2)}) collective-permute-start(bf16[1024,128]{1,0:T(8,128)(2,1)S(1)} %collective-permute-done.1.refs_2_), channel_id=1, source_target_pairs={{0,8},{8,0},{16,24},{24,16},{1,9},{9,1},{17,25},{25,17},{2,10},{10... | collective-permute-start | bytes 786440 | tf_op jit(solution)/shard_map/ppermute | solution.py:448
  53.6 1.2 %copy-start = (bf16[16,128,256]{2,1,0:T(8,128)(2,1)S(1)}, bf16[16,128,256]{2,1,0:T(8,128)(2,1)}, u32[]{:S(2)}) copy-start(bf16[16,128,256]{2,1,0:T(8,128)(2,1)} %relayout.1.cot_ref) | copy-start | bytes 3145732
  61.8 18.1 %all-to-all-start.2 = ((bf16[8,16,2048]{2,1,0:T(8,128)(2,1)}), bf16[8,16,2048]{2,1,0:T(8,128)(2,1)S(1)}, u32[]{:S(2)}, u32[]{:S(2)}) async-start(bf16[8,16,2048]{2,1,0:T(8,128)(2,1)} %bitcast.8), calls=%async_computation.2 | async-start | bytes 1048576 | tf_op jit(solution)/shard_map/all_to_all | solution.py:503
  65.4 1.2 %collective-permute-start.3 = (f32[64,64]{1,0:T(8,128)S(1)}, f32[64,64]{1,0:T(8,128)S(1)}, u32[]{:S(2)}, u32[]{:S(2)}) collective-permute-start(f32[64,64]{1,0:T(8,128)S(1)} %get-tuple-element.31), channel_id=1, source_target_pairs={{0,8},{8,0},{16,24},{24,16},{1,9},{9,1},{17,25},{25,17},{2,10},{10... | collective-permute-start | bytes 49160 | tf_op jit(solution)/shard_map/ppermute | solution.py:448
  66.7 3.9 %collective-permute-start.4 = (f32[64,64]{1,0:T(8,128)S(1)}, f32[64,64]{1,0:T(8,128)S(1)}, u32[]{:S(2)}, u32[]{:S(2)}) collective-permute-start(f32[64,64]{1,0:T(8,128)S(1)} %add.14), channel_id=1, source_target_pairs={{0,16},{8,24},{16,0},{24,8},{1,17},{9,25},{17,1},{25,9},{2,18},{10... | collective-permute-start | bytes 49160 | tf_op jit(solution)/shard_map/ppermute | solution.py:448
  80.5 1.7 %copy-start.2 = (bf16[1024,128]{1,0:T(8,128)(2,1)}, bf16[1024,128]{1,0:T(8,128)(2,1)S(1)}, u32[]{:S(2)}) copy-start(bf16[1024,128]{1,0:T(8,128)(2,1)S(1)} %grad_spectra.1.rest_0_.refs_4_) | copy-start | bytes 786436
  80.5 11.1 %collective-permute-start.5 = (bf16[1024,128]{1,0:T(8,128)(2,1)S(1)}, bf16[1024,128]{1,0:T(8,128)(2,1)S(1)}, u32[]{:S(2)}, u32[]{:S(2)}) collective-permute-start(bf16[1024,128]{1,0:T(8,128)(2,1)S(1)} %grad_spectra.1.rest_0_.refs_4_), channel_id=1, source_target_pairs={{0,8},{8,0},{16,24},{24,16},{1,9},{9,1},{17,25},{25,17},{2,10},{10... | collective-permute-start | bytes 786440 | tf_op jit(solution)/shard_map/ppermute | solution.py:448
  80.6 11.1 %collective-permute-start.6 = (bf16[1024,128]{1,0:T(8,128)(2,1)S(1)}, bf16[1024,128]{1,0:T(8,128)(2,1)S(1)}, u32[]{:S(2)}, u32[]{:S(2)}) collective-permute-start(bf16[1024,128]{1,0:T(8,128)(2,1)S(1)} %grad_spectra.1.rest_0_.refs_4_), channel_id=1, source_target_pairs={{0,16},{8,24},{16,0},{24,8},{1,17},{9,25},{17,1},{25,9},{2,18},{10... | collective-permute-start | bytes 786440 | tf_op jit(solution)/shard_map/ppermute | solution.py:448
  91.7 5.2 %copy-start.9 = (bf16[1024,128]{1,0:T(8,128)(2,1)}, bf16[1024,128]{1,0:T(8,128)(2,1)S(1)}, u32[]{:S(2)}) copy-start(bf16[1024,128]{1,0:T(8,128)(2,1)S(1)} %collective-permute-done.5.refs_5_) | copy-start | bytes 786436
  91.7 5.2 %copy-start.10 = (bf16[1024,128]{1,0:T(8,128)(2,1)}, bf16[1024,128]{1,0:T(8,128)(2,1)S(1)}, u32[]{:S(2)}) copy-start(bf16[1024,128]{1,0:T(8,128)(2,1)S(1)} %collective-permute-done.6.refs_6_) | copy-start | bytes 786436
  91.7 22.5 %all-to-all-start.3 = ((bf16[8,32,1152]{2,1,0:T(8,128)(2,1)}), bf16[8,32,1152]{2,1,0:T(8,128)(2,1)S(1)}, u32[]{:S(2)}, u32[]{:S(2)}) async-start(bf16[8,32,1152]{2,1,0:T(8,128)(2,1)} %bitcast.28), calls=%async_computation.3 | async-start | bytes 1179648 | tf_op jit(solution)/shard_map/all_to_all | solution.py:503
  95.3 1.6 %collective-permute-start.7 = (bf16[1024,128]{1,0:T(8,128)(2,1)S(1)}, bf16[1024,128]{1,0:T(8,128)(2,1)S(1)}, u32[]{:S(2)}, u32[]{:S(2)}) collective-permute-start(bf16[1024,128]{1,0:T(8,128)(2,1)S(1)} %collective-permute-done.6.refs_6_), channel_id=1, source_target_pairs={{0,8},{8,0},{16,24},{24,16},{1,9},{9,1},{17,25},{25,17},{2,10},{10... | collective-permute-start | bytes 786440 | tf_op jit(solution)/shard_map/ppermute | solution.py:448
  96.9 0.7 copy-start.11
